TPU v7x, 512 devices: a whole 4x4x16 slice. The times are simulated.
512 devices in a mesh: row: 128 (over y_hi, x, z), head: 4 (over y_lo, core).
Axes of the slice: x: 4, y: 4 (y_hi: 2, y_lo: 2; y = y_hi * 2 + y_lo), z: 16, core: 2. Of those that a mesh axis runs over, the one named last changes fastest.
Arguments:
- pair: bfloat16 [512, 512, 128], P('row', None, 'head'), may hold values from -100 to 100
- w_query: bfloat16 [128, 128], P(None, 'head'), may hold values from -0.5 to 0.5
- w_key: bfloat16 [128, 128], P(None, 'head'), may hold values from -0.5 to 0.5
- w_value: bfloat16 [128, 128], P(None, 'head'), may hold values from -0.5 to 0.5
- w_gate: bfloat16 [128, 128], P(None, 'head'), may hold values from -0.5 to 0.5
- w_bias: bfloat16 [128, 4], P(None, 'head')
- w_out: bfloat16 [128, 128], replicated, may hold values from -0.5 to 0.5
- intra_chain_logit_shift: float32 [4], P('head'), may hold values from -2 to 2
- block_lists: int32 [8, 2], replicated, may hold values from 0 to 7, as said below
- chain_ids: int32 [512], replicated, may hold values from 0 to 3, never falling along the last dimension, each value on 1 to 256 neighbouring positions
Outputs:
- attended: bfloat16 [512, 512, 128], P(None, ('row', 'head'))
Inputs may be any that keep to these rules, and one draw needn't show every extreme that they name: `block_lists`: each query block b lists 2 distinct key blocks in rising order, b itself among them.
All inputs are finite; a program needn't handle non-finite values.
Results may differ from a plain program's by a relative error of at most 0.012.
The roundings to bfloat16 on the way count: a program that leaves them out, or rounds other values in their place, can miss the bound.
Values may be sent and summed in bfloat16 or wider, within the bound.
No kernel may reach another device: no remote copies, remote signals or barrier semaphores. Data moves between devices by JAX's collectives and lax.ppermute only.
A program may use at most 64 MiB of HBM per device.

v0:
```python
import math

import jax
import jax.numpy as jnp
from jax import lax
from jax.sharding import PartitionSpec as P


def local(
    pair,
    w_query,
    w_key,
    w_value,
    w_gate,
    w_bias,
    w_out,
    intra_chain_logit_shift,
    block_lists,
    chain_ids,
):
    rows_here, width, part_chan = pair.shape
    n_head = lax.axis_size("head")
    head_dim = w_query.shape[1]
    channels = w_out.shape[1]
    nblk, kblk = block_lists.shape
    blk = width // nblk
    w_cat = jnp.concatenate([w_query, w_key, w_value, w_gate], axis=1)
    piece = lax.all_gather(pair, "head", axis=2, tiled=True)
    count = piece.shape[2]
    flat = piece.reshape(-1, count)
    projected = jnp.dot(flat, w_cat, preferred_element_type=jnp.float32)
    bias_col = jnp.dot(flat, w_bias, preferred_element_type=jnp.float32)
    projected = projected.astype(jnp.bfloat16).reshape(rows_here, width, 4, head_dim)
    bias_rows = bias_col.astype(jnp.bfloat16).reshape(rows_here, width)
    key_pos = (
        block_lists[:, :, None] * blk + jnp.arange(blk, dtype=jnp.int32)[None, None, :]
    ).reshape(nblk, kblk * blk)
    plane = lax.all_gather(bias_rows, "row", axis=0, tiled=True)
    picked = jnp.take_along_axis(
        plane.reshape(nblk, blk, nblk, blk), block_lists[:, None, :, None], axis=2
    )
    picked = picked.reshape(nblk, blk, kblk * blk)
    same = chain_ids.reshape(nblk, blk)[:, :, None] == jnp.take(chain_ids, key_pos)[:, None, :]
    logit_bias = picked.astype(jnp.float32) + intra_chain_logit_shift[0] * same.astype(jnp.float32)
    logit_scale = 1.0 / math.sqrt(head_dim)

    def one_row(row):
        query_rows = row[:, 0].reshape(nblk, blk, head_dim)
        key_rows = jnp.take(row[:, 1], key_pos, axis=0)
        value_rows = jnp.take(row[:, 2], key_pos, axis=0)
        scores = (
            jnp.einsum("cxr,cur->cxu", query_rows, key_rows, preferred_element_type=jnp.float32)
            * logit_scale
            + logit_bias
        )
        top = jnp.max(scores, axis=-1, keepdims=True)
        expo = jnp.exp(scores - top)
        attention_weight = (expo / jnp.sum(expo, axis=-1, keepdims=True)).astype(jnp.bfloat16)
        mixed = jnp.einsum(
            "cpx,cxe->cpe", attention_weight, value_rows, preferred_element_type=jnp.float32
        ).reshape(width, head_dim)
        return (jax.nn.sigmoid(row[:, 3].astype(jnp.float32)) * mixed).astype(jnp.bfloat16)

    gated = lax.map(one_row, projected)
    col_count = rows_here // n_head
    moved = lax.all_to_all(
        lax.all_to_all(gated, "row", split_axis=1, concat_axis=0, tiled=True),
        "head",
        split_axis=1,
        concat_axis=2,
        tiled=True,
    )
    moved = moved.reshape(width * col_count, n_head * head_dim)
    result = jnp.dot(moved, w_out, preferred_element_type=jnp.float32).astype(jnp.bfloat16)
    return result.reshape(width, col_count, channels)


def solution(mesh):
    in_specs = (
        P("row", None, "head"),
        P(None, "head"),
        P(None, "head"),
        P(None, "head"),
        P(None, "head"),
        P(None, "head"),
        P(),
        P("head"),
        P(),
        P(),
    )
    out_specs = P(None, ("row", "head"), None)
    return jax.shard_map(local, mesh=mesh, in_specs=in_specs, out_specs=out_specs, check_vma=False)
```

profile of v0, /device:TPU:1, one launch (start us, length us, event | category | flops | bytes accessed | tf_op | source)
XLA Modules:
  0.0 454.4 jit_solution(16103097847711542261)
XLA Ops:
  0.0 0.8 copy.57
  1.0 0.6 copy-done.7
  1.7 0.6 copy-done.1
  2.4 6.9 %gather_fusion.2 = s32[1024]{0:T(1024)S(1)} fusion(s32[512]{0:T(512)S(1)} %copy-done.1, s32[1024]{0:T(1024)S(1)} %fusion.28), kind=kCustom, calls=%fused_computation.2 | custom fusion | bytes 12288 | tf_op jit(solution)/shard_map/jit(_take)/gather | solution.py:43
  9.4 13.2 %all_gather.6 = bf16[4,512,128]{1,0,2:T(4,128)(2,1)S(1)} all-gather(bf16[4,512,32]{1,0,2:T(4,128)(2,1)S(1)} %copy.51), channel_id=1, replica_groups=mesh['row'=128,'head'=4] {'head'}, dimensions={2}, use_global_device_ids=true | all-gather | bytes 655360 | tf_op jit(solution)/shard_map/all_gather | solution.py:28
  23.1 0.6 copy-done.8
  24.0 303.7 %all-gather = bf16[128,4,512]{2,1,0:T(4,128)(2,1)S(1)} all-gather(bf16[1,4,512]{2,1,0:T(4,128)(2,1)S(1)} %reshape.239), channel_id=1, replica_groups=mesh['row'=128,'head'=4] {'row'}, dimensions={0}, use_global_device_ids=true | all-gather | bytes 528384 | tf_op jit(solution)/shard_map/all_gather | solution.py:38
  328.6 0.6 gather_fusion.3
  331.5 35.8 %while.11 = (s32[]{:T(128)}, bf16[4,512,32]{2,1,0:T(8,128)(2,1)S(1)}, bf16[4,512,4,32]{1,0,3,2:T(4,128)(2,1)S(1)}, f32[8,64,128]{2,1,0:T(8,128)S(1)}, s32[8,2]{1,0:T(8,128)S(1)}, /*index=5*/s32[128]{0:T(128)S(1)}, s32[]{:T(128)}) while((s32[]{:T(128)}, bf16[4,512,32]{2,1,0:T(8,128)(2,1)S(1)}, ...), condition=%wide.region_3.5_spmd.clone, body=%wide.region_0.4_spmd.clone.sunk | while | flops 9024256 | bytes 3088533 | solution.py:64
  332.3 3.2 gather_fusion
  336.1 3.2 gather_fusion.1
  339.4 0.9 fusion.56
  341.2 3.2 gather_fusion
  345.0 3.2 gather_fusion.1
  348.4 0.9 fusion.56
  350.2 3.2 gather_fusion
  354.0 3.2 gather_fusion.1
  357.3 0.9 fusion.56
  359.1 3.2 gather_fusion
  362.9 3.2 gather_fusion.1
  366.3 0.9 fusion.56
  368.0 21.8 %all_to_all.27 = bf16[128,2,256]{2,1,0:T(2,128)(2,1)S(1)} all-to-all(bf16[128,2,256]{2,1,0:T(2,128)(2,1)S(1)} %reshape.255), channel_id=1, replica_groups=mesh['row'=128,'head'=4] {'row'}, dimensions={0} | all-to-all | bytes 262144 | tf_op jit(solution)/shard_map/all_to_all | solution.py:67
  390.5 63.0 %all_to_all.28 = bf16[512,4,32]{0,2,1:T(8,128)(2,1)S(1)} all-to-all(bf16[512,4,32]{0,2,1:T(8,128)(2,1)S(1)} %copy.61), channel_id=1, replica_groups=mesh['row'=128,'head'=4] {'head'}, dimensions={1} | all-to-all | bytes 262144 | tf_op jit(solution)/shard_map/all_to_all | solution.py:66
  453.5 0.9 fusion.19
  (97 shorter events, 11.2 us)
Async XLA Ops:
  0.0 453.5 %copy-start = (bf16[128,128]{1,0:T(8,128)(2,1)S(1)}, bf16[128,128]{1,0:T(8,128)(2,1)}, u32[]{:S(2)}) copy-start(bf16[128,128]{1,0:T(8,128)(2,1)} %param.20) | copy-start | bytes 98308
  0.9 0.7 copy-start.7
  1.6 0.7 copy-start.1
  2.4 6.9 %copy-start.2 = (bf16[4,512,32]{1,2,0:T(8,128)(2,1)S(1)}, bf16[4,512,32]{1,2,0:T(8,128)(2,1)}, u32[]{:S(2)}) copy-start(bf16[4,512,32]{1,2,0:T(8,128)(2,1)} %param.14) | copy-start | bytes 393220
  23.0 0.7 copy-start.8
  329.5 1.1 copy-start.4
  329.5 1.1 copy-start.5
  329.5 1.1 copy-start.6
  329.7 1.0 copy-start.3
where the time goes:
time: 455 us; the launch traced here: 454 us
  blocking collectives  402 us (88%)
  local copies, waits for them, and re-layouts  44.1 us (10%)
  matrix products  5.74 us (1%)
    all_gather x1, blocking collectives, local(): plane = lax.all_gather(bias_rows, 'row', axis=0, tiled=True)  304 us
    all_to_all x1, blocking collectives, local(): lax.all_to_all(lax.all_to_all(gated, 'row', split_axis=1, concat_axis=0,...  63 us
    all_to_all x1, blocking collectives, local(): lax.all_to_all(gated, 'row', split_axis=1, concat_axis=0, tiled=True)  21.8 us
    gather x8, local copies, waits for them, and re-layouts, one_row(): value_rows = jnp.take(row[:, 2], key_pos, axis=0)  13.3 us
    gather x8, local copies, waits for them, and re-layouts, one_row(): key_rows = jnp.take(row[:, 1], key_pos, axis=0)  13.3 us
    all_gather x1, blocking collectives, local(): piece = lax.all_gather(pair, 'head', axis=2, tiled=True)  13.2 us

commit v1 on v0

v1 whole, which is shorter than its diff:
```python
import functools
import math

import jax
import jax.numpy as jnp
from jax import lax
from jax.experimental import pallas as pl
from jax.experimental.pallas import tpu as pltpu
from jax.sharding import PartitionSpec as P

F32, BF16 = jnp.float32, jnp.bfloat16
VMEM = pl.BlockSpec(memory_space=pltpu.VMEM)
SMEM = pl.BlockSpec(memory_space=pltpu.SMEM)
LIMIT = 24 * 1024 * 1024
BLK, NBLK, HEADS, HD, C, N = 64, 8, 4, 32, 128, 512
ROWS = 4
QB = 16


def nt(a, b):
    return lax.dot_general(a, b, (((1,), (1,)), ((), ())), preferred_element_type=F32)


def nn(a, b):
    return jnp.dot(a, b, preferred_element_type=F32)


def iota(shape, dim):
    return lax.broadcasted_iota(jnp.int32, shape, dim)


def pack_kernel(pair, wq, wk, wv, wg, wb, shift, out):
    h = lax.axis_index("head")
    out[0:128, :] = pair[...].reshape(128, N)
    out[128:160, 0:128] = wq[...]
    out[128:160, 128:256] = wk[...]
    out[128:160, 256:384] = wv[...]
    out[128:160, 384:512] = wg[...]
    s = jnp.full((16, 128), shift[0], F32)
    hi = s.astype(BF16).astype(F32)
    mid = (s - hi).astype(BF16).astype(F32)
    low = s - hi - mid
    w = jnp.broadcast_to(wb[...].astype(F32), (16, 128))
    row = iota((16, 128), 0)
    part = row // 4
    value = jnp.where(part == 0, w, jnp.where(part == 1, hi, jnp.where(part == 2, mid, low)))
    value = jnp.where(row % 4 == h, value, 0.0)
    out[160:176, 0:128] = value.astype(BF16)
    out[160:176, 128:512] = jnp.zeros((16, 384), BF16)


def heads_small(g):
    small = g[0, 160:176, 0:128].astype(F32)
    for k in range(1, HEADS):
        small = small + g[k, 160:176, 0:128].astype(F32)
    return small


def pick(first, second, b0, b1):
    lane = iota(first.shape, 1)
    first = jnp.where(b0 % 2 == 0, first, pltpu.roll(first, 64, 1))
    second = jnp.where(b1 % 2 == 1, second, pltpu.roll(second, 64, 1))
    return jnp.where(lane < 64, first, second)


def bias_kernel(lists, g, out):
    h = lax.axis_index("head")
    b = lax.axis_index("row") // 16
    small = heads_small(g).astype(BF16)
    found = []
    for s in range(2):
        chunk = pl.multiple_of(lists[b, s] // 2 * 128, 128)
        z = jnp.concatenate(
            [g[k, pl.ds(pl.multiple_of(h * 32, 32), 32), pl.ds(chunk, 128)] for k in range(HEADS)], axis=0
        )
        found.append(nn(small, z))
    both = pick(found[0], found[1], lists[b, 0], lists[b, 1])[0:4]
    tile = jnp.concatenate([both] * 4, axis=0).astype(BF16)
    for r in range(32):
        out[r * 16 : (r + 1) * 16, :] = tile


def score_kernel(lists, chain, g, s_out, v_out, g_out, k_scr):
    h = lax.axis_index("head")
    small = heads_small(g)
    sel = (iota((128, N), 1) == 4 * iota((128, N), 0) + h).astype(BF16)
    wT = jnp.concatenate([g[k, 128:160, :] for k in range(HEADS)], axis=0)
    w_qg = jnp.concatenate([wT[:, 0:128], wT[:, 384:512]], axis=0)
    w_kv = wT[:, 128:384]
    w_kv = jnp.concatenate([w_kv[:, 0:128], w_kv[:, 128:256]], axis=0)
    chain_q = nt(sel, jnp.broadcast_to(chain[...].astype(F32).astype(BF16), (128, N)))
    scale = 1.0 / math.sqrt(HD)
    lane16 = iota((QB, 128), 1) // HD
    same = []
    for b in range(NBLK):
        b0, b1 = lists[b, 0], lists[b, 1]
        c0 = chain[:, pl.ds(pl.multiple_of(b0 // 2 * 128, 128), 128)].astype(F32)
        c1 = chain[:, pl.ds(pl.multiple_of(b1 // 2 * 128, 128), 128)].astype(F32)
        ck = pick(jnp.broadcast_to(c0, (8, 128)), jnp.broadcast_to(c1, (8, 128)), b0, b1)[0:1]
        same.append(chain_q[b * QB : (b + 1) * QB] == ck)
    shifts = [small[4 + k : 5 + k] + small[8 + k : 9 + k] + small[12 + k : 13 + k] for k in range(HEADS)]
    for i in range(ROWS):
        zt = jnp.concatenate([g[k, i * 32 : (i + 1) * 32, :] for k in range(HEADS)], axis=0)
        z = zt.T
        kv = nt(z, w_kv).astype(BF16)
        k_scr[i] = kv[:, 0:128]
        v_out[i] = kv[:, 128:256]
        zq = nt(sel, zt).astype(BF16)
        qg = nt(zq, w_qg).astype(BF16)
        g_out[i] = qg[:, 128:256]
        q = qg[:, 0:128]
        for b in range(NBLK):
            q16 = q[b * QB : (b + 1) * QB]
            zero = jnp.zeros_like(q16)
            qbd = jnp.concatenate([jnp.where(lane16 == k, q16, zero) for k in range(HEADS)], axis=0)
            kb = jnp.concatenate(
                [k_scr[i, pl.ds(pl.multiple_of(lists[b, s] * BLK, BLK), BLK), :] for s in range(2)], axis=0
            )
            s64 = nt(qbd, kb) * scale
            for k in range(HEADS):
                s_out[i, b, k * QB : (k + 1) * QB, :] = s64[k * QB : (k + 1) * QB] + jnp.where(same[b], shifts[k], 0.0)


def mix_kernel(lists, bias, s_in, v, gate, w_out, out, acc):
    perm = (iota((64, 64), 1) == (iota((64, 64), 0) % QB) * 4 + iota((64, 64), 0) // QB).astype(BF16)
    lane16 = iota((QB, 128), 1) // HD
    for b in range(NBLK):
        bias_b = nn(perm, bias[b * 64 : (b + 1) * 64, :])
        for i in range(ROWS):
            s = s_in[i, b] + bias_b
            e = jnp.exp(s - jnp.max(s, axis=-1, keepdims=True))
            p = (e * (1.0 / jnp.sum(e, axis=-1, keepdims=True))).astype(BF16)
            vb = jnp.concatenate(
                [v[i, pl.ds(pl.multiple_of(lists[b, t] * BLK, BLK), BLK), :] for t in range(2)], axis=0
            )
            o64 = nn(p, vb)
            o = o64[0:QB]
            for k in range(1, HEADS):
                o = jnp.where(lane16 == k, o64[k * QB : (k + 1) * QB], o)
            gated = jax.nn.sigmoid(gate[i, b * QB : (b + 1) * QB, :].astype(F32)) * o
            acc[pl.ds(b * 64 + i, QB, stride=4), :] = gated
    out[...] = nn(acc[...].astype(BF16), w_out[...]).astype(BF16)


def call(kernel, ins, outs, scratch=(), flops=0, nbytes=0):
    return pl.pallas_call(
        kernel,
        in_specs=ins,
        out_specs=[VMEM] * len(outs) if isinstance(outs, list) else VMEM,
        out_shape=outs,
        scratch_shapes=list(scratch),
        compiler_params=pltpu.CompilerParams(vmem_limit_bytes=LIMIT),
        cost_estimate=pl.CostEstimate(flops=flops, bytes_accessed=nbytes, transcendentals=0),
    )


def local(pair, w_query, w_key, w_value, w_gate, w_bias, w_out, shift, block_lists, chain_ids):
    shape = jax.ShapeDtypeStruct
    packed = call(pack_kernel, [VMEM] * 6 + [SMEM], shape((176, N), BF16), nbytes=400000)(
        pair.transpose(0, 2, 1), w_query.T, w_key.T, w_value.T, w_gate.T, w_bias.T, shift
    )
    g = lax.all_gather(packed, "head", axis=0)
    mine = call(bias_kernel, [SMEM, VMEM], shape((512, 128), BF16), nbytes=400000)(block_lists, g)
    bias = lax.all_to_all(mine.reshape(128, 4, 128), "row", 0, 0, tiled=True).reshape(512, 128)
    scores, v, gate = call(
        score_kernel,
        [SMEM, VMEM, VMEM],
        [shape((ROWS, NBLK, 64, 128), F32), shape((ROWS, N, 128), BF16), shape((ROWS, 128, 128), BF16)],
        [pltpu.VMEM((ROWS, N, 128), BF16)],
        flops=1000000000,
        nbytes=4000000,
    )(block_lists, chain_ids.reshape(1, N), g)
    mixed = call(
        mix_kernel,
        [SMEM] + [VMEM] * 5,
        shape((512, 128), BF16),
        [pltpu.VMEM((512, 128), F32)],
        flops=100000000,
        nbytes=3000000,
    )(block_lists, bias, scores, v, gate, w_out)
    moved = lax.all_to_all(mixed.reshape(128, 4, 128), "row", 0, 0, tiled=True)
    return moved.reshape(512, 1, 128)


def solution(mesh):
    in_specs = (
        P("row", None, "head"),
        P(None, "head"),
        P(None, "head"),
        P(None, "head"),
        P(None, "head"),
        P(None, "head"),
        P(),
        P("head"),
        P(),
        P(),
    )
    out_specs = P(None, ("row", "head"), None)
    return jax.shard_map(local, mesh=mesh, in_specs=in_specs, out_specs=out_specs, check_vma=False)
```

time: 455 us -> 84.4 us (0.19)
  the two profiles are of different devices: /device:TPU:1 before, /device:TPU:2 now
where the time goes in v1:
time: 84.4 us; the launch traced here: 84 us
  blocking collectives  33.1 us (39%)
  starting transfers between devices  21.9 us (26%)
  waiting for transfers between devices  16.4 us (19%)
  Pallas kernels  7.48 us (9%)
  local copies, waits for them, and re-layouts  4.38 us (5%)
    all_to_all x1, blocking collectives, local(): moved = lax.all_to_all(mixed.reshape(128, 4, 128), 'row', 0, 0, tiled=True)  24.8 us
    all_to_all x1, starting transfers between devices, local(): lax.all_to_all(mine.reshape(128, 4, 128), 'row', 0, 0, tiled=True)  21.9 us
    all_to_all x1, waiting for transfers between devices, local(): lax.all_to_all(mine.reshape(128, 4, 128), 'row', 0, 0, tiled=True)  16.4 us
    all_gather x1, blocking collectives, local(): g = lax.all_gather(packed, 'head', axis=0)  8.33 us
    unnamed x18, local copies, waits for them, and re-layouts  4.38 us
    pallas_call x1, Pallas kernels, local(): call(mix_kernel, [SMEM] + [VMEM] * 5, shape((512, 128), BF16), [pltpu.VME...  3.32 us
    pallas_call x1, Pallas kernels, local(): call(score_kernel, [SMEM, VMEM, VMEM], [shape((ROWS, NBLK, 64, 128), F32)...  2.65 us
  transfers between devices with their start and end apart: 1, of which 1 were waited for; matrix products, arithmetic and copies ran while one was open for 0% of the time, Pallas kernels for 3%

profile of v1, /device:TPU:2, one launch (start us, length us, event | category | flops | bytes accessed | tf_op | source)
XLA Modules:
  0.0 84.0 jit_solution(7934695173780601838)
XLA Ops:
  0.0 0.0 copy-start.2
  0.0 0.0 copy-start.3
  0.0 0.8 copy.13.lists
  1.4 0.0 copy-start.6
  1.4 0.0 copy-done.2
  1.5 0.0 copy-done.3
  1.5 0.6 copy-done.6
  2.1 0.0 copy-start
  2.1 0.9 %copy-done = bf16[4,512,32]{1,2,0:T(8,128)(2,1)S(1)} copy-done((bf16[4,512,32]{1,2,0:T(8,128)(2,1)S(1)}, bf16[4,512,32]{1,2,0:T(8,128)(2,1)}, u32[]{:S(2)}) %copy-start) | copy-done | bytes 131096
  3.0 0.0 copy-start.4
  3.0 0.7 copy-done.4
  3.7 0.0 copy-start.5
  3.7 0.7 copy-done.5
  4.4 8.3 %all-gather = bf16[704,512]{1,0:T(8,128)(2,1)S(1)} all-gather(bf16[176,512]{1,0:T(8,128)(2,1)S(1)} %shard_map.100), channel_id=2, replica_groups=mesh['row'=128,'head'=4] {'head'}, dimensions={0}, use_global_device_ids=true | all-gather | bytes 901120 | tf_op jit(solution)/shard_map/all_gather | solution.py:162
  12.7 1.5 %shard_map.101 = bf16[512,128]{1,0:T(8,128)(2,1)} custom-call(s32[8,2]{1,0:T(8,128)S(1)} %copy.13.lists, bf16[4,176,512]{2,1,0:T(8,128)(2,1)S(1)} %bitcast.12), custom_call_target="tpu_custom_call" | custom-call | bytes 400000 | tf_op jit(solution)/shard_map/pallas_call | solution.py:163
  14.2 21.9 %all-to-all-start = ((bf16[128,4,128]{2,1,0:T(4,128)(2,1)}), bf16[128,4,128]{2,1,0:T(4,128)(2,1)S(1)}, u32[]{:S(2)}, u32[]{:S(2)}) async-start(bf16[128,4,128]{2,1,0:T(4,128)(2,1)} %bitcast.7), calls=%async_computation | async-start | bytes 262144 | tf_op jit(solution)/shard_map/all_to_all | solution.py:164
  36.2 0.0 copy-done.7
  36.2 0.0 copy-start.1
  36.2 2.6 %shard_map.102 = (f32[4,8,64,128]{3,2,1,0:T(8,128)S(1)}, bf16[4,512,128]{2,1,0:T(8,128)(2,1)S(1)}, bf16[4,128,128]{2,1,0:T(8,128)(2,1)S(1)}) custom-call(s32[8,2]{1,0:T(8,128)S(1)} %copy.13.lists, s32[1,512]{1,0:T(1,128)S(1)} %bitcast.22, bf16[4,176,512]{2,1,0:T(8,128)(2,1)S(1)} %bitcast.13), custom_call_target="tpu_custom_call" | custom-call | flops 1000000000 | bytes 4000000 | tf_op jit(solution)/shard_map/pallas_call | solution.py:165
  38.8 16.4 %all-to-all-done = bf16[128,4,128]{2,1,0:T(4,128)(2,1)S(1)} async-done(((bf16[128,4,128]{2,1,0:T(4,128)(2,1)}), bf16[128,4,128]{2,1,0:T(4,128)(2,1)S(1)}, u32[]{:S(2)}, u32[]{:S(2)}) %all-to-all-start) | async-done | bytes 131104 | tf_op jit(solution)/shard_map/all_to_all | solution.py:164
  55.3 0.0 copy-done.1
  55.3 3.3 %shard_map.103 = bf16[512,128]{1,0:T(8,128)(2,1)S(1)} custom-call(s32[8,2]{1,0:T(8,128)S(1)} %copy.13.lists, bf16[512,128]{1,0:T(8,128)(2,1)S(1)} %bitcast.14, f32[4,8,64,128]{3,2,1,0:T(8,128)S(1)} %get-tuple-element.8.s_in, bf16[4,512,128]{2,1,0:T(8,128)(2,1)S(1)} %get-tuple-element.9.v, bf16[4,128,128]{2,1,0:T(8,128)(2,1)S(1)} %get-tuple-element.10.gate, ...), custom_call_target="tpu_custom_call" | custom-call | flops 100000000 | bytes 3000000 | tf_op jit(solution)/shard_map/pallas_call | solution.py:173
  58.6 24.8 %all_to_all.10 = bf16[128,4,128]{2,1,0:T(4,128)(2,1)S(1)} all-to-all(bf16[128,4,128]{2,1,0:T(4,128)(2,1)S(1)} %bitcast.15), channel_id=1, replica_groups=mesh['row'=128,'head'=4] {'row'}, dimensions={0} | all-to-all | bytes 262144 | tf_op jit(solution)/shard_map/all_to_all | solution.py:181
  83.3 0.7 copy.16
  (2 shorter events, 0.0 us)
Async XLA Ops:
  0.0 1.4 %copy-start.2 = (bf16[128,32]{0,1:T(8,128)(2,1)S(1)}, bf16[128,32]{0,1:T(8,128)(2,1)}, u32[]{:S(2)}) copy-start(bf16[128,32]{0,1:T(8,128)(2,1)} %param.11) | copy-start | bytes 24580
  0.0 1.5 %copy-start.3 = (bf16[128,32]{0,1:T(8,128)(2,1)S(1)}, bf16[128,32]{0,1:T(8,128)(2,1)}, u32[]{:S(2)}) copy-start(bf16[128,32]{0,1:T(8,128)(2,1)} %param.12) | copy-start | bytes 24580
  1.4 0.7 copy-start.6
  2.1 0.9 %copy-start = (bf16[4,512,32]{1,2,0:T(8,128)(2,1)S(1)}, bf16[4,512,32]{1,2,0:T(8,128)(2,1)}, u32[]{:S(2)}) copy-start(bf16[4,512,32]{1,2,0:T(8,128)(2,1)} %param.10) | copy-start | bytes 393220
  3.0 0.7 copy-start.4
  3.7 0.7 copy-start.5
  14.2 21.9 %copy-start.7 = (s32[512]{0:T(512)S(1)}, s32[512]{0:T(512)}, u32[]{:S(2)}) copy-start(s32[512]{0:T(512)} %param.19) | copy-start | bytes 6148
  14.2 41.0 %all-to-all-start = ((bf16[128,4,128]{2,1,0:T(4,128)(2,1)}), bf16[128,4,128]{2,1,0:T(4,128)(2,1)S(1)}, u32[]{:S(2)}, u32[]{:S(2)}) async-start(bf16[128,4,128]{2,1,0:T(4,128)(2,1)} %bitcast.7), calls=%async_computation | async-start | bytes 262144 | tf_op jit(solution)/shard_map/all_to_all | solution.py:164
  36.2 19.1 %copy-start.1 = (bf16[128,128]{1,0:T(8,128)(2,1)S(1)}, bf16[128,128]{1,0:T(8,128)(2,1)}, u32[]{:S(2)}) copy-start(bf16[128,128]{1,0:T(8,128)(2,1)} %w_out.1) | copy-start | bytes 98308

commit v2 on v0

v2 whole, which is shorter than its diff:
```python
import math

import jax
import jax.numpy as jnp
import numpy as np
from jax import lax
from jax.experimental import pallas as pl
from jax.experimental.pallas import tpu as pltpu
from jax.sharding import PartitionSpec as P

F32, BF16 = jnp.float32, jnp.bfloat16
VMEM = pl.BlockSpec(memory_space=pltpu.VMEM)
HBM = pl.BlockSpec(memory_space=pltpu.HBM)
LIMIT = 24 * 1024 * 1024
HEADS, HD, N = 4, 32, 512
DEVICES = np.arange(512).reshape(8, 16, 2, 2)
OVER_BLOCK = DEVICES.transpose(1, 3, 0, 2).reshape(32, 16).tolist()
OVER_Z = DEVICES.transpose(0, 3, 1, 2).reshape(16, 32).tolist()
OVER_CORE = [[0, 1], [2, 3]]
Q, I = 32, 16
MSG = 96


def nt(a, b):
    return lax.dot_general(a, b, (((1,), (1,)), ((), ())), preferred_element_type=F32)


def nn(a, b):
    return jnp.dot(a, b, preferred_element_type=F32)


def iota(shape, dim):
    return lax.broadcasted_iota(jnp.int32, shape, dim)


def place():
    row, head = lax.axis_index("row"), lax.axis_index("head")
    return row // 16, head // 2, head % 2, head


def pack_kernel(pair, wq, wk, wv, wg, wb, chain, lists, shift, out, same_out, sel_out, x, w, wb_v, chain_v, halves, sem):
    b, _, core, head = place()
    copies = [
        pltpu.make_async_copy(pair, x, sem.at[0]),
        pltpu.make_async_copy(wq, w.at[0:32], sem.at[1]),
        pltpu.make_async_copy(wk, w.at[32:64], sem.at[2]),
        pltpu.make_async_copy(wv, w.at[64:96], sem.at[3]),
        pltpu.make_async_copy(wg, w.at[96:128], sem.at[4]),
        pltpu.make_async_copy(wb, wb_v, sem.at[5]),
        pltpu.make_async_copy(chain, chain_v, sem.at[6]),
    ]
    for copy in copies:
        copy.start()
    for copy in copies:
        copy.wait()
    s = jnp.full((16, 128), shift[0], F32)
    hi = s.astype(BF16).astype(F32)
    mid = (s - hi).astype(BF16).astype(F32)
    low = s - hi - mid
    wide = jnp.broadcast_to(wb_v[...].astype(F32), (16, 128))
    row = iota((16, 128), 0)
    part = row // 4
    small = jnp.where(part == 0, wide, jnp.where(part == 1, hi, jnp.where(part == 2, mid, low)))
    small = jnp.where(row % 4 == head, small, 0.0).astype(BF16)
    w_part = w[pl.ds(pl.multiple_of(b * 16, 16), 16), :]
    flat = x[...].reshape(128, N)
    halves[0] = flat
    for c in range(4):
        halves[1, :, c * 128 : (c + 1) * 128] = pltpu.roll(flat[:, c * 128 : (c + 1) * 128].astype(F32), 64, 1).astype(BF16)
    lane = iota((128, 128), 1)
    for d in range(8):
        b0, b1 = lists[0, d], lists[1, d]
        first = halves[b0 % 2, :, pl.ds(pl.multiple_of(b0 // 2 * 128, 128), 128)]
        second = halves[1 - b1 % 2, :, pl.ds(pl.multiple_of(b1 // 2 * 128, 128), 128)]
        keys = jnp.where(lane < 64, first, second)
        for y in range(2):
            at = (2 * d + y) * MSG
            out[at : at + 64] = keys[y * 64 : (y + 1) * 64]
            out[at + 64 : at + 80] = w_part
            out[at + 80 : at + 96] = small
    b0, b1 = lists[0, b], lists[1, b]
    c0 = jnp.broadcast_to(chain_v[:, pl.ds(pl.multiple_of(b0 // 2 * 128, 128), 128)].astype(F32), (Q, 128))
    c1 = jnp.broadcast_to(chain_v[:, pl.ds(pl.multiple_of(b1 // 2 * 128, 128), 128)].astype(F32), (Q, 128))
    c0 = jnp.where(b0 % 2 == 0, c0, pltpu.roll(c0, 64, 1))
    c1 = jnp.where(b1 % 2 == 1, c1, pltpu.roll(c1, 64, 1))
    key_chain = jnp.where(iota((Q, 128), 1) < 64, c0, c1)
    own = jnp.where(b0 == b, 0, 64)
    sel = iota((Q, 128), 1) == own + 2 * iota((Q, 128), 0) + core
    query_chain = jnp.sum(jnp.where(sel, key_chain, 0.0), axis=-1, keepdims=True)
    same_out[...] = (query_chain == key_chain).astype(F32)
    sel_out[...] = sel.astype(BF16)


def heads_small(g):
    return sum(g[c, y, 80:96, :].astype(F32) for c in range(2) for y in range(2))


def bias_kernel(g, out):
    b, _, core, _ = place()
    z = jnp.concatenate(
        [g[k % 2, 2 * b + k // 2, pl.ds(pl.multiple_of(core * 32, 32), 32), :] for k in range(HEADS)], axis=0
    )
    found = nn(heads_small(g).astype(BF16), z)[0:4]
    tile = jnp.concatenate([found] * 4, axis=0).astype(BF16)
    for r in range(8):
        out[r * 16 : (r + 1) * 16, :] = tile


def score_kernel(g, same, sel, s_out, v_out, gate_out, zq_scr, k_scr):
    small = heads_small(g)
    scale = 1.0 / math.sqrt(HD)
    selector = sel[...]
    w = [
        jnp.concatenate([g[k % 2, 2 * s + k // 2, 64:80, :] for k in range(HEADS) for s in (2 * t, 2 * t + 1)], axis=0)
        for t in range(4)
    ]
    w_kv = jnp.concatenate([w[1], w[2]], axis=0)
    w_qg = jnp.concatenate([w[0], w[3]], axis=0)
    for i in range(I):
        s, t = i // 2, i % 2
        zt = jnp.concatenate([g[k % 2, 2 * s + k // 2, t * 32 : (t + 1) * 32, :] for k in range(HEADS)], axis=0)
        kv = nn(w_kv, zt).astype(BF16)
        k_scr[i] = kv[0:128]
        v_out[i] = kv[128:256]
        zq_scr[i * Q : (i + 1) * Q] = nt(selector, zt).astype(BF16)
    qg = nt(zq_scr[...], w_qg).astype(BF16)
    gate_out[...] = qg[:, 128:256]
    head_of_lane = iota((Q, 128), 1) // HD
    moved = jnp.concatenate(
        [same[...] * (small[4 + k : 5 + k] + small[8 + k : 9 + k] + small[12 + k : 13 + k]) for k in range(HEADS)], axis=0
    )
    for i in range(I):
        q = qg[i * Q : (i + 1) * Q, 0:128]
        zero = jnp.zeros_like(q)
        q_all = jnp.concatenate([jnp.where(head_of_lane == k, q, zero) for k in range(HEADS)], axis=0)
        s_out[i] = nn(q_all, k_scr[i]) * scale + moved


def mix_kernel(bias, s_in, v, gate, w_out, out, acc):
    perm = (iota((128, 128), 1) == (iota((128, 128), 0) % Q) * 4 + iota((128, 128), 0) // Q).astype(BF16)
    head_of_lane = iota((Q, 128), 1) // HD
    plane = nn(perm, bias[...])
    for i in range(I):
        s = s_in[i] + plane
        e = jnp.exp(s - jnp.max(s, axis=-1, keepdims=True))
        p = (e * (1.0 / jnp.sum(e, axis=-1, keepdims=True))).astype(BF16)
        every = nt(p, v[i])
        o = every[0:Q]
        for k in range(1, HEADS):
            o = jnp.where(head_of_lane == k, every[k * Q : (k + 1) * Q], o)
        acc[pl.ds(i, Q, stride=I), :] = jax.nn.sigmoid(gate[i * Q : (i + 1) * Q, :].astype(F32)) * o
    out[...] = nn(acc[...].astype(BF16), w_out[...]).astype(BF16)


def order_kernel(moved, out, before, after):
    before[...] = moved[...].astype(F32)
    for s in range(8):
        for t in range(2):
            after[pl.ds(s * 64 + t, 32, stride=2), :] = before[pl.ds(2 * s + t, 32, stride=16), :]
    out[...] = after[...].astype(BF16)


def call(kernel, ins, outs, scratch=(), flops=0, nbytes=0, limit=LIMIT):
    return pl.pallas_call(
        kernel,
        in_specs=ins,
        out_specs=[VMEM] * len(outs) if isinstance(outs, list) else VMEM,
        out_shape=outs,
        scratch_shapes=list(scratch),
        compiler_params=pltpu.CompilerParams(vmem_limit_bytes=limit),
        cost_estimate=pl.CostEstimate(flops=flops, bytes_accessed=nbytes, transcendentals=0),
    )


def local(pair, w_query, w_key, w_value, w_gate, w_bias, w_out, shift, block_lists, chain_ids):
    shape = jax.ShapeDtypeStruct
    smem = pl.BlockSpec(memory_space=pltpu.SMEM)
    packed, same, sel = call(
        pack_kernel,
        [HBM] * 7 + [smem] * 2,
        [shape((16 * MSG, 128), BF16), shape((Q, 128), F32), shape((Q, 128), BF16)],
        [
            pltpu.VMEM((4, 32, N), BF16),
            pltpu.VMEM((128, 128), BF16),
            pltpu.VMEM((1, 128), BF16),
            pltpu.VMEM((1, N), jnp.int32),
            pltpu.VMEM((2, 128, N), BF16),
            pltpu.SemaphoreType.DMA((7,)),
        ],
        nbytes=1000000,
        limit=None,
    )(
        pair.transpose(0, 2, 1), w_query.T, w_key.T, w_value.T, w_gate.T, w_bias.T,
        chain_ids.reshape(1, N), block_lists.T, shift,
    )
    got = lax.all_to_all(
        packed.reshape(16, MSG, 128), ("row", "head"), 0, 0, tiled=True, axis_index_groups=OVER_BLOCK
    )
    g = lax.all_gather(got, "head", axis=0, axis_index_groups=OVER_CORE)
    mine = call(bias_kernel, [VMEM], shape((128, 128), BF16), nbytes=400000)(g)
    bias = lax.all_to_all(
        mine.reshape(32, 4, 128), ("row", "head"), 0, 0, tiled=True, axis_index_groups=OVER_Z
    ).reshape(128, 128)
    scores, v, gate = call(
        score_kernel,
        [VMEM] * 3,
        [shape((I, 128, 128), F32), shape((I, 128, 128), BF16), shape((I * Q, 128), BF16)],
        [pltpu.VMEM((I * Q, 128), BF16), pltpu.VMEM((I, 128, 128), BF16)],
        flops=1000000000,
        nbytes=4000000,
    )(g, same, sel)
    mixed = call(
        mix_kernel,
        [VMEM] * 5,
        shape((I * Q, 128), BF16),
        [pltpu.VMEM((I * Q, 128), F32)],
        flops=100000000,
        nbytes=3000000,
    )(bias, scores, v, gate, w_out)
    moved = lax.all_to_all(
        mixed.reshape(32, I, 128), ("row", "head"), 0, 0, tiled=True, axis_index_groups=OVER_Z
    ).reshape(512, 128)
    ordered = call(
        order_kernel, [VMEM], shape((512, 128), BF16), [pltpu.VMEM((512, 128), F32)] * 2, nbytes=300000
    )(moved)
    return ordered.reshape(512, 1, 128)


def solution(mesh):
    in_specs = (
        P("row", None, "head"),
        P(None, "head"),
        P(None, "head"),
        P(None, "head"),
        P(None, "head"),
        P(None, "head"),
        P(),
        P("head"),
        P(),
        P(),
    )
    out_specs = P(None, ("row", "head"), None)
    return jax.shard_map(local, mesh=mesh, in_specs=in_specs, out_specs=out_specs, check_vma=False)
```

time: 455 us -> 73 us (0.16)
  the two profiles are of different devices: /device:TPU:1 before, /device:TPU:8 now
where the time goes in v2:
time: 73 us; the launch traced here: 72.6 us
  blocking collectives  38.4 us (53%)
  starting transfers between devices  15.7 us (22%)
  waiting for transfers between devices  11.4 us (16%)
  Pallas kernels  6.33 us (9%)
    all_to_all x1, blocking collectives, local(): lax.all_to_all(mixed.reshape(32, I, 128), ('row', 'head'), 0, 0, tiled=Tr...  19 us
    all_to_all x1, blocking collectives, local(): lax.all_to_all(packed.reshape(16, MSG, 128), ('row', 'head'), 0, 0, tiled...  17 us
    all_to_all x1, starting transfers between devices, local(): lax.all_to_all(mine.reshape(32, 4, 128), ('row', 'head'), 0, 0, tiled=Tru...  15.7 us
    all_to_all x1, waiting for transfers between devices, local(): lax.all_to_all(mine.reshape(32, 4, 128), ('row', 'head'), 0, 0, tiled=Tru...  11.4 us
    pallas_call x1, Pallas kernels, local(): call(pack_kernel, [HBM] * 7 + [smem] * 2, [shape((16 * MSG, 128), BF16),...  2.63 us
    all_gather x1, blocking collectives, local(): g = lax.all_gather(got, 'head', axis=0, axis_index_groups=OVER_CORE)  2.36 us
  transfers between devices with their start and end apart: 1, of which 1 were waited for; matrix products, arithmetic and copies ran while one was open for 0% of the time, Pallas kernels for 1%

profile of v2, /device:TPU:8, one launch (start us, length us, event | category | flops | bytes accessed | tf_op | source)
XLA Modules:
  0.0 72.6 jit_solution(9625169677864346108)
XLA Ops:
  0.7 2.6 %shard_map.100 = (bf16[1536,128]{1,0:T(8,128)(2,1)}, f32[32,128]{1,0:T(8,128)}, bf16[32,128]{1,0:T(8,128)(2,1)}) custom-call(bf16[4,32,512]{2,1,0:T(8,128)(2,1)} %bitcast.21, bf16[32,128]{1,0:T(8,128)(2,1)} %bitcast.22, bf16[32,128]{1,0:T(8,128)(2,1)} %bitcast.23, bf16[32,128]{1,0:T(8,128)(2,1)} %bitcast.24, bf16[32,128]{1,0:T(8,128)(2,1)} %bitcast.25, ...), custom_call_target="tpu_custom_call" | custom-call | bytes 1000000 | tf_op jit(solution)/shard_map/pallas_call | solution.py:178
  3.3 17.0 %all_to_all.15 = bf16[16,96,128]{2,1,0:T(8,128)(2,1)S(1)} all-to-all(bf16[16,96,128]{2,1,0:T(8,128)(2,1)} %bitcast.20), channel_id=1, replica_groups={{0,2,64,66,128,130,192,194,256,258,320,322,384,386,448,450},{1,3,65,67,..., dimensions={0} | all-to-all | bytes 786432 | tf_op jit(solution)/shard_map/all_to_all | solution.py:196
  20.3 2.4 %all-gather = bf16[32,96,128]{2,1,0:T(8,128)(2,1)S(1)} all-gather(bf16[16,96,128]{2,1,0:T(8,128)(2,1)S(1)} %all_to_all.15), channel_id=2, replica_groups={{0,1},{2,3},{4,5},{6,7},{8,9},{10,11},{12,13},{14,15},{16,17},{18,19},{..., dimensions={0}, use_global_device_ids=true | all-gather | bytes 1179648 | tf_op jit(solution)/shard_map/all_gather | solution.py:199
  22.7 0.8 %shard_map.101 = bf16[128,128]{1,0:T(8,128)(2,1)} custom-call(bf16[2,16,96,128]{3,2,1,0:T(8,128)(2,1)S(1)} %bitcast.15), custom_call_target="tpu_custom_call" | custom-call | bytes 400000 | tf_op jit(solution)/shard_map/pallas_call | solution.py:200
  23.4 0.0 copy-start.1
  23.4 0.0 copy-start.2
  23.4 15.7 %all-to-all-start.1 = ((bf16[32,4,128]{2,1,0:T(4,128)(2,1)}), bf16[32,4,128]{2,1,0:T(4,128)(2,1)S(1)}, u32[]{:S(2)}, u32[]{:S(2)}) async-start(bf16[32,4,128]{2,1,0:T(4,128)(2,1)} %bitcast.10), calls=%async_computation.1 | async-start | bytes 65536 | tf_op jit(solution)/shard_map/all_to_all | solution.py:201
  39.1 0.0 copy-done.1
  39.1 0.0 copy-done.2
  39.1 0.0 copy-start
  39.1 1.0 %shard_map.102 = (f32[16,128,128]{2,1,0:T(8,128)S(1)}, bf16[16,128,128]{2,1,0:T(8,128)(2,1)S(1)}, bf16[512,128]{1,0:T(8,128)(2,1)S(1)}) custom-call(bf16[2,16,96,128]{3,2,1,0:T(8,128)(2,1)S(1)} %bitcast.16, f32[32,128]{1,0:T(8,128)S(1)} %copy-done.1, bf16[32,128]{1,0:T(8,128)(2,1)S(1)} %copy-done.2), custom_call_target="tpu_custom_call" | custom-call | flops 1000000000 | bytes 4000000 | tf_op jit(solution)/shard_map/pallas_call | solution.py:204
  40.2 11.4 %all-to-all-done.1 = bf16[32,4,128]{2,1,0:T(4,128)(2,1)S(1)} async-done(((bf16[32,4,128]{2,1,0:T(4,128)(2,1)}), bf16[32,4,128]{2,1,0:T(4,128)(2,1)S(1)}, u32[]{:S(2)}, u32[]{:S(2)}) %all-to-all-start.1) | async-done | bytes 32800 | tf_op jit(solution)/shard_map/all_to_all | solution.py:201
  51.6 0.0 copy-done
  51.6 1.2 %shard_map.103 = bf16[512,128]{1,0:T(8,128)(2,1)S(1)} custom-call(bf16[128,128]{1,0:T(8,128)(2,1)S(1)} %bitcast.19, f32[16,128,128]{2,1,0:T(8,128)S(1)} %get-tuple-element.14.s_in, bf16[16,128,128]{2,1,0:T(8,128)(2,1)S(1)} %get-tuple-element.15.v, bf16[512,128]{1,0:T(8,128)(2,1)S(1)} %get-tuple-element.16.gate, bf16[128,128]{1,0:T(8,128)(2,1)S(1)} %copy-done), custom_call_target="tpu_custom_call" | custom-call | flops 100000000 | bytes 3000000 | tf_op jit(solution)/shard_map/pallas_call | solution.py:212
  52.8 19.0 %all_to_all.16 = bf16[32,16,128]{2,1,0:T(8,128)(2,1)S(1)} all-to-all(bf16[32,16,128]{2,1,0:T(8,128)(2,1)S(1)} %bitcast.18), channel_id=1, replica_groups={{0,2,4,6,8,10,12,14,16,18,20,22,24,26,28,30,32,34,36,38,40,42,44,46,48,..., dimensions={0} | all-to-all | bytes 262144 | tf_op jit(solution)/shard_map/all_to_all | solution.py:220
  71.8 0.8 %shard_map.104 = bf16[512,128]{1,0:T(8,128)(2,1)} custom-call(bf16[512,128]{1,0:T(8,128)(2,1)S(1)} %bitcast.17), custom_call_target="tpu_custom_call" | custom-call | bytes 300000 | tf_op jit(solution)/shard_map/pallas_call | solution.py:223
Async XLA Ops:
  23.4 15.7 %copy-start.1 = (f32[32,128]{1,0:T(8,128)S(1)}, f32[32,128]{1,0:T(8,128)}, u32[]{:S(2)}) copy-start(f32[32,128]{1,0:T(8,128)} %get-tuple-element.12.same) | copy-start | bytes 49156
  23.4 15.7 %copy-start.2 = (bf16[32,128]{1,0:T(8,128)(2,1)S(1)}, bf16[32,128]{1,0:T(8,128)(2,1)}, u32[]{:S(2)}) copy-start(bf16[32,128]{1,0:T(8,128)(2,1)} %get-tuple-element.13.sel) | copy-start | bytes 24580
  23.4 28.2 %all-to-all-start.1 = ((bf16[32,4,128]{2,1,0:T(4,128)(2,1)}), bf16[32,4,128]{2,1,0:T(4,128)(2,1)S(1)}, u32[]{:S(2)}, u32[]{:S(2)}) async-start(bf16[32,4,128]{2,1,0:T(4,128)(2,1)} %bitcast.10), calls=%async_computation.1 | async-start | bytes 65536 | tf_op jit(solution)/shard_map/all_to_all | solution.py:201
  39.1 12.5 %copy-start = (bf16[128,128]{1,0:T(8,128)(2,1)S(1)}, bf16[128,128]{1,0:T(8,128)(2,1)}, u32[]{:S(2)}) copy-start(bf16[128,128]{1,0:T(8,128)(2,1)} %w_out.1) | copy-start | bytes 98308

commit v3 on v2

--- a/solution.py
+++ b/solution.py
@@ -14,8 +14,11 @@
 LIMIT = 24 * 1024 * 1024
 HEADS, HD, N = 4, 32, 512
 DEVICES = np.arange(512).reshape(8, 16, 2, 2)
-OVER_BLOCK = DEVICES.transpose(1, 3, 0, 2).reshape(32, 16).tolist()
-OVER_Z = DEVICES.transpose(0, 3, 1, 2).reshape(16, 32).tolist()
+FAR = 6
+OVER_BLOCK = DEVICES[np.arange(8) ^ FAR].transpose(1, 3, 0, 2).reshape(32, 16).tolist()
+TURN_BIAS, TURN_OUT = 8, 8
+OVER_Z_BIAS = np.roll(DEVICES, -TURN_BIAS, 1).transpose(0, 3, 1, 2).reshape(16, 32).tolist()
+OVER_Z_OUT = np.roll(DEVICES, -TURN_OUT, 1).transpose(0, 3, 1, 2).reshape(16, 32).tolist()
 OVER_CORE = [[0, 1], [2, 3]]
 Q, I = 32, 16
 MSG = 96
@@ -38,22 +41,47 @@
     return row // 16, head // 2, head % 2, head
 
 
-def pack_kernel(pair, wq, wk, wv, wg, wb, chain, lists, shift, out, same_out, sel_out, x, w, wb_v, chain_v, halves, sem):
+def pack_kernel(
+    pair, wq, wk, wv, wg, wb, chain, lists_in, shift_in,
+    out, same_out, sel_out,
+    x, w, wb_v, chain_v, lists, shift, halves, message, same_v, sel_v, sem,
+):
     b, _, core, head = place()
     copies = [
-        pltpu.make_async_copy(pair, x, sem.at[0]),
-        pltpu.make_async_copy(wq, w.at[0:32], sem.at[1]),
-        pltpu.make_async_copy(wk, w.at[32:64], sem.at[2]),
-        pltpu.make_async_copy(wv, w.at[64:96], sem.at[3]),
-        pltpu.make_async_copy(wg, w.at[96:128], sem.at[4]),
-        pltpu.make_async_copy(wb, wb_v, sem.at[5]),
-        pltpu.make_async_copy(chain, chain_v, sem.at[6]),
+        pltpu.make_async_copy(lists_in, lists, sem.at[0]),
+        pltpu.make_async_copy(chain, chain_v, sem.at[1]),
+        pltpu.make_async_copy(shift_in, shift, sem.at[2]),
+        pltpu.make_async_copy(wb, wb_v, sem.at[3]),
+        pltpu.make_async_copy(pair, x, sem.at[4]),
+        pltpu.make_async_copy(wq, w.at[0:32], sem.at[5]),
+        pltpu.make_async_copy(wk, w.at[32:64], sem.at[6]),
+        pltpu.make_async_copy(wv, w.at[64:96], sem.at[7]),
+        pltpu.make_async_copy(wg, w.at[96:128], sem.at[8]),
     ]
     for copy in copies:
         copy.start()
-    for copy in copies:
+    copies[0].wait()
+    copies[1].wait()
+    b0, b1 = lists[0, b], lists[1, b]
+    c0 = jnp.broadcast_to(chain_v[:, pl.ds(pl.multiple_of(b0 // 2 * 128, 128), 128)].astype(F32), (Q, 128))
+    c1 = jnp.broadcast_to(chain_v[:, pl.ds(pl.multiple_of(b1 // 2 * 128, 128), 128)].astype(F32), (Q, 128))
+    c0 = jnp.where(b0 % 2 == 0, c0, pltpu.roll(c0, 64, 1))
+    c1 = jnp.where(b1 % 2 == 1, c1, pltpu.roll(c1, 64, 1))
+    key_chain = jnp.where(iota((Q, 128), 1) < 64, c0, c1)
+    own = jnp.where(b0 == b, 0, 64)
+    sel = iota((Q, 128), 1) == own + (2 * iota((Q, 128), 0) + 4 * TURN_OUT) % 64 + core
+    query_chain = jnp.sum(jnp.where(sel, key_chain, 0.0), axis=-1, keepdims=True)
+    same_v[...] = (query_chain == key_chain).astype(F32)
+    sel_v[...] = sel.astype(BF16)
+    sent = [
+        pltpu.make_async_copy(same_v, same_out, sem.at[9]),
+        pltpu.make_async_copy(sel_v, sel_out, sem.at[10]),
+    ]
+    for copy in sent:
+        copy.start()
+    for copy in copies[2:]:
         copy.wait()
-    s = jnp.full((16, 128), shift[0], F32)
+    s = jnp.broadcast_to(shift[...], (16, 128))
     hi = s.astype(BF16).astype(F32)
     mid = (s - hi).astype(BF16).astype(F32)
     low = s - hi - mid
@@ -73,22 +101,17 @@
         first = halves[b0 % 2, :, pl.ds(pl.multiple_of(b0 // 2 * 128, 128), 128)]
         second = halves[1 - b1 % 2, :, pl.ds(pl.multiple_of(b1 // 2 * 128, 128), 128)]
         keys = jnp.where(lane < 64, first, second)
+        start = 2 * (d ^ FAR) * MSG
         for y in range(2):
-            at = (2 * d + y) * MSG
-            out[at : at + 64] = keys[y * 64 : (y + 1) * 64]
-            out[at + 64 : at + 80] = w_part
-            out[at + 80 : at + 96] = small
-    b0, b1 = lists[0, b], lists[1, b]
-    c0 = jnp.broadcast_to(chain_v[:, pl.ds(pl.multiple_of(b0 // 2 * 128, 128), 128)].astype(F32), (Q, 128))
-    c1 = jnp.broadcast_to(chain_v[:, pl.ds(pl.multiple_of(b1 // 2 * 128, 128), 128)].astype(F32), (Q, 128))
-    c0 = jnp.where(b0 % 2 == 0, c0, pltpu.roll(c0, 64, 1))
-    c1 = jnp.where(b1 % 2 == 1, c1, pltpu.roll(c1, 64, 1))
-    key_chain = jnp.where(iota((Q, 128), 1) < 64, c0, c1)
-    own = jnp.where(b0 == b, 0, 64)
-    sel = iota((Q, 128), 1) == own + 2 * iota((Q, 128), 0) + core
-    query_chain = jnp.sum(jnp.where(sel, key_chain, 0.0), axis=-1, keepdims=True)
-    same_out[...] = (query_chain == key_chain).astype(F32)
-    sel_out[...] = sel.astype(BF16)
+            at = start + y * MSG
+            message[at : at + 64] = keys[y * 64 : (y + 1) * 64]
+            message[at + 64 : at + 80] = w_part
+            message[at + 80 : at + 96] = small
+        span = pl.ds(start, 2 * MSG)
+        sent.append(pltpu.make_async_copy(message.at[span], out.at[span], sem.at[11 + d]))
+        sent[-1].start()
+    for copy in sent:
+        copy.wait()
 
 
 def heads_small(g):
@@ -98,7 +121,7 @@
 def bias_kernel(g, out):
     b, _, core, _ = place()
     z = jnp.concatenate(
-        [g[k % 2, 2 * b + k // 2, pl.ds(pl.multiple_of(core * 32, 32), 32), :] for k in range(HEADS)], axis=0
+        [g[k % 2, 2 * (b ^ FAR) + k // 2, pl.ds(pl.multiple_of(core * 32, 32), 32), :] for k in range(HEADS)], axis=0
     )
     found = nn(heads_small(g).astype(BF16), z)[0:4]
     tile = jnp.concatenate([found] * 4, axis=0).astype(BF16)
@@ -111,14 +134,14 @@
     scale = 1.0 / math.sqrt(HD)
     selector = sel[...]
     w = [
-        jnp.concatenate([g[k % 2, 2 * s + k // 2, 64:80, :] for k in range(HEADS) for s in (2 * t, 2 * t + 1)], axis=0)
+        jnp.concatenate([g[k % 2, 2 * (s ^ FAR) + k // 2, 64:80, :] for k in range(HEADS) for s in (2 * t, 2 * t + 1)], axis=0)
         for t in range(4)
     ]
     w_kv = jnp.concatenate([w[1], w[2]], axis=0)
     w_qg = jnp.concatenate([w[0], w[3]], axis=0)
     for i in range(I):
         s, t = i // 2, i % 2
-        zt = jnp.concatenate([g[k % 2, 2 * s + k // 2, t * 32 : (t + 1) * 32, :] for k in range(HEADS)], axis=0)
+        zt = jnp.concatenate([g[k % 2, 2 * (s ^ FAR) + k // 2, t * 32 : (t + 1) * 32, :] for k in range(HEADS)], axis=0)
         kv = nn(w_kv, zt).astype(BF16)
         k_scr[i] = kv[0:128]
         v_out[i] = kv[128:256]
@@ -137,7 +160,9 @@
 
 
 def mix_kernel(bias, s_in, v, gate, w_out, out, acc):
-    perm = (iota((128, 128), 1) == (iota((128, 128), 0) % Q) * 4 + iota((128, 128), 0) // Q).astype(BF16)
+    row = iota((128, 128), 0)
+    peer = (row % Q + 2 * (TURN_OUT - TURN_BIAS)) % Q
+    perm = (iota((128, 128), 1) == peer * 4 + row // Q).astype(BF16)
     head_of_lane = iota((Q, 128), 1) // HD
     plane = nn(perm, bias[...])
     for i in range(I):
@@ -156,42 +181,48 @@
     before[...] = moved[...].astype(F32)
     for s in range(8):
         for t in range(2):
-            after[pl.ds(s * 64 + t, 32, stride=2), :] = before[pl.ds(2 * s + t, 32, stride=16), :]
+            n = 2 * TURN_OUT
+            after[pl.ds(s * 64 + 2 * n + t, 32 - n, stride=2), :] = before[pl.ds(2 * s + t, 32 - n, stride=16), :]
+            after[pl.ds(s * 64 + t, n, stride=2), :] = before[pl.ds((32 - n) * 16 + 2 * s + t, n, stride=16), :]
     out[...] = after[...].astype(BF16)
 
 
-def call(kernel, ins, outs, scratch=(), flops=0, nbytes=0, limit=LIMIT):
+def call(kernel, ins, outs, scratch=(), flops=0, nbytes=0):
     return pl.pallas_call(
         kernel,
         in_specs=ins,
         out_specs=[VMEM] * len(outs) if isinstance(outs, list) else VMEM,
         out_shape=outs,
         scratch_shapes=list(scratch),
-        compiler_params=pltpu.CompilerParams(vmem_limit_bytes=limit),
+        compiler_params=pltpu.CompilerParams(vmem_limit_bytes=LIMIT),
         cost_estimate=pl.CostEstimate(flops=flops, bytes_accessed=nbytes, transcendentals=0),
     )
 
 
 def local(pair, w_query, w_key, w_value, w_gate, w_bias, w_out, shift, block_lists, chain_ids):
     shape = jax.ShapeDtypeStruct
-    smem = pl.BlockSpec(memory_space=pltpu.SMEM)
-    packed, same, sel = call(
+    packed, same, sel = pl.pallas_call(
         pack_kernel,
-        [HBM] * 7 + [smem] * 2,
-        [shape((16 * MSG, 128), BF16), shape((Q, 128), F32), shape((Q, 128), BF16)],
-        [
+        in_specs=[HBM] * 9,
+        out_specs=[HBM] * 3,
+        out_shape=[shape((16 * MSG, 128), BF16), shape((Q, 128), F32), shape((Q, 128), BF16)],
+        scratch_shapes=[
             pltpu.VMEM((4, 32, N), BF16),
             pltpu.VMEM((128, 128), BF16),
             pltpu.VMEM((1, 128), BF16),
             pltpu.VMEM((1, N), jnp.int32),
+            pltpu.SMEM((2, 8), jnp.int32),
+            pltpu.VMEM((1, 1), F32),
             pltpu.VMEM((2, 128, N), BF16),
-            pltpu.SemaphoreType.DMA((7,)),
+            pltpu.VMEM((16 * MSG, 128), BF16),
+            pltpu.VMEM((Q, 128), F32),
+            pltpu.VMEM((Q, 128), BF16),
+            pltpu.SemaphoreType.DMA((19,)),
         ],
-        nbytes=1000000,
-        limit=None,
+        cost_estimate=pl.CostEstimate(flops=0, bytes_accessed=1000000, transcendentals=0),
     )(
         pair.transpose(0, 2, 1), w_query.T, w_key.T, w_value.T, w_gate.T, w_bias.T,
-        chain_ids.reshape(1, N), block_lists.T, shift,
+        chain_ids.reshape(1, N), block_lists.T, shift.reshape(1, 1),
     )
     got = lax.all_to_all(
         packed.reshape(16, MSG, 128), ("row", "head"), 0, 0, tiled=True, axis_index_groups=OVER_BLOCK
@@ -199,7 +230,7 @@
     g = lax.all_gather(got, "head", axis=0, axis_index_groups=OVER_CORE)
     mine = call(bias_kernel, [VMEM], shape((128, 128), BF16), nbytes=400000)(g)
     bias = lax.all_to_all(
-        mine.reshape(32, 4, 128), ("row", "head"), 0, 0, tiled=True, axis_index_groups=OVER_Z
+        mine.reshape(32, 4, 128), ("row", "head"), 0, 0, tiled=True, axis_index_groups=OVER_Z_BIAS
     ).reshape(128, 128)
     scores, v, gate = call(
         score_kernel,
@@ -218,7 +249,7 @@
         nbytes=3000000,
     )(bias, scores, v, gate, w_out)
     moved = lax.all_to_all(
-        mixed.reshape(32, I, 128), ("row", "head"), 0, 0, tiled=True, axis_index_groups=OVER_Z
+        mixed.reshape(32, I, 128), ("row", "head"), 0, 0, tiled=True, axis_index_groups=OVER_Z_OUT
     ).reshape(512, 128)
     ordered = call(
         order_kernel, [VMEM], shape((512, 128), BF16), [pltpu.VMEM((512, 128), F32)] * 2, nbytes=300000

time: 73 us -> 65 us (0.89)
  the two profiles are of different devices: /device:TPU:8 before, /device:TPU:1 now
where the time goes in v3:
time: 65 us; the launch traced here: 64.5 us
  blocking collectives  39.3 us (60%)
  starting transfers between devices  16.6 us (26%)
  Pallas kernels  5.69 us (9%)
  waiting for transfers between devices  2.15 us (3%)
  between operations  0.71 us (1%)
    all_to_all x1, blocking collectives, local(): lax.all_to_all(mixed.reshape(32, I, 128), ('row', 'head'), 0, 0, tiled=Tr...  18.8 us
    all_to_all x1, starting transfers between devices, local(): lax.all_to_all(mine.reshape(32, 4, 128), ('row', 'head'), 0, 0, tiled=Tru...  16.6 us
    all_to_all x1, blocking collectives, local(): lax.all_to_all(packed.reshape(16, MSG, 128), ('row', 'head'), 0, 0, tiled...  13.1 us
    all_gather x1, blocking collectives, local(): g = lax.all_gather(got, 'head', axis=0, axis_index_groups=OVER_CORE)  7.37 us
    all_to_all x1, waiting for transfers between devices, local(): lax.all_to_all(mine.reshape(32, 4, 128), ('row', 'head'), 0, 0, tiled=Tru...  2.15 us
    pallas_call x1, Pallas kernels, local(): pl.pallas_call(pack_kernel, in_specs=[HBM] * 9, out_specs=[HBM] * 3, out_...  2 us
  transfers between devices with their start and end apart: 1, of which 1 were waited for; matrix products, arithmetic and copies ran while one was open for 0% of the time, Pallas kernels for 2%

profile of v3, /device:TPU:1, one launch (start us, length us, event | category | flops | bytes accessed | tf_op | source)
XLA Modules:
  0.0 64.5 jit_solution(8683243549606305322)
XLA Ops:
  0.7 2.0 %shard_map.100 = (bf16[1536,128]{1,0:T(8,128)(2,1)}, f32[32,128]{1,0:T(8,128)}, bf16[32,128]{1,0:T(8,128)(2,1)}) custom-call(bf16[4,32,512]{2,1,0:T(8,128)(2,1)} %bitcast.23, bf16[32,128]{1,0:T(8,128)(2,1)} %bitcast.24, bf16[32,128]{1,0:T(8,128)(2,1)} %bitcast.25, bf16[32,128]{1,0:T(8,128)(2,1)} %bitcast.26, bf16[32,128]{1,0:T(8,128)(2,1)} %bitcast.27, ...), custom_call_target="tpu_custom_call" | custom-call | bytes 1000000 | tf_op jit(solution)/shard_map/pallas_call | solution.py:204
  2.7 13.1 %all_to_all.15 = bf16[16,96,128]{2,1,0:T(8,128)(2,1)S(1)} all-to-all(bf16[16,96,128]{2,1,0:T(8,128)(2,1)} %bitcast.22), channel_id=1, replica_groups={{384,386,448,450,256,258,320,322,128,130,192,194,0,2,64,66},{385,387,44..., dimensions={0} | all-to-all | bytes 786432 | tf_op jit(solution)/shard_map/all_to_all | solution.py:227
  15.8 7.4 %all-gather = bf16[32,96,128]{2,1,0:T(8,128)(2,1)S(1)} all-gather(bf16[16,96,128]{2,1,0:T(8,128)(2,1)S(1)} %all_to_all.15), channel_id=2, replica_groups={{0,1},{2,3},{4,5},{6,7},{8,9},{10,11},{12,13},{14,15},{16,17},{18,19},{..., dimensions={0}, use_global_device_ids=true | all-gather | bytes 1179648 | tf_op jit(solution)/shard_map/all_gather | solution.py:230
  23.2 0.8 %shard_map.101 = bf16[128,128]{1,0:T(8,128)(2,1)} custom-call(bf16[2,16,96,128]{3,2,1,0:T(8,128)(2,1)S(1)} %bitcast.17), custom_call_target="tpu_custom_call" | custom-call | bytes 400000 | tf_op jit(solution)/shard_map/pallas_call | solution.py:231
  23.9 0.0 copy-start.1
  23.9 0.0 copy-start.2
  23.9 16.6 %all-to-all-start.1 = ((bf16[32,4,128]{2,1,0:T(4,128)(2,1)}), bf16[32,4,128]{2,1,0:T(4,128)(2,1)S(1)}, u32[]{:S(2)}, u32[]{:S(2)}) async-start(bf16[32,4,128]{2,1,0:T(4,128)(2,1)} %bitcast.11), calls=%async_computation.1 | async-start | bytes 65536 | tf_op jit(solution)/shard_map/all_to_all | solution.py:232
  40.6 0.0 copy-done.1
  40.6 0.0 copy-done.2
  40.6 0.0 copy-start
  40.6 1.0 %shard_map.102 = (f32[16,128,128]{2,1,0:T(8,128)S(1)}, bf16[16,128,128]{2,1,0:T(8,128)(2,1)S(1)}, bf16[512,128]{1,0:T(8,128)(2,1)S(1)}) custom-call(bf16[2,16,96,128]{3,2,1,0:T(8,128)(2,1)S(1)} %bitcast.18, f32[32,128]{1,0:T(8,128)S(1)} %copy-done.1, bf16[32,128]{1,0:T(8,128)(2,1)S(1)} %copy-done.2), custom_call_target="tpu_custom_call" | custom-call | flops 1000000000 | bytes 4000000 | tf_op jit(solution)/shard_map/pallas_call | solution.py:235
  41.6 2.2 %all-to-all-done.1 = bf16[32,4,128]{2,1,0:T(4,128)(2,1)S(1)} async-done(((bf16[32,4,128]{2,1,0:T(4,128)(2,1)}), bf16[32,4,128]{2,1,0:T(4,128)(2,1)S(1)}, u32[]{:S(2)}, u32[]{:S(2)}) %all-to-all-start.1) | async-done | bytes 32800 | tf_op jit(solution)/shard_map/all_to_all | solution.py:232
  43.8 0.0 copy-done
  43.8 1.2 %shard_map.103 = bf16[512,128]{1,0:T(8,128)(2,1)S(1)} custom-call(bf16[128,128]{1,0:T(8,128)(2,1)S(1)} %bitcast.21, f32[16,128,128]{2,1,0:T(8,128)S(1)} %get-tuple-element.14.s_in, bf16[16,128,128]{2,1,0:T(8,128)(2,1)S(1)} %get-tuple-element.15.v, bf16[512,128]{1,0:T(8,128)(2,1)S(1)} %get-tuple-element.16.gate, bf16[128,128]{1,0:T(8,128)(2,1)S(1)} %copy-done), custom_call_target="tpu_custom_call" | custom-call | flops 100000000 | bytes 3000000 | tf_op jit(solution)/shard_map/pallas_call | solution.py:243
  44.9 18.8 %all_to_all.16 = bf16[32,16,128]{2,1,0:T(8,128)(2,1)S(1)} all-to-all(bf16[32,16,128]{2,1,0:T(8,128)(2,1)S(1)} %bitcast.20), channel_id=1, replica_groups={{32,34,36,38,40,42,44,46,48,50,52,54,56,58,60,62,0,2,4,6,8,10,12,14,16,..., dimensions={0} | all-to-all | bytes 262144 | tf_op jit(solution)/shard_map/all_to_all | solution.py:251
  63.7 0.8 %shard_map.104 = bf16[512,128]{1,0:T(8,128)(2,1)} custom-call(bf16[512,128]{1,0:T(8,128)(2,1)S(1)} %bitcast.19), custom_call_target="tpu_custom_call" | custom-call | bytes 300000 | tf_op jit(solution)/shard_map/pallas_call | solution.py:254
Async XLA Ops:
  23.9 16.7 %copy-start.1 = (f32[32,128]{1,0:T(8,128)S(1)}, f32[32,128]{1,0:T(8,128)}, u32[]{:S(2)}) copy-start(f32[32,128]{1,0:T(8,128)} %get-tuple-element.12.same) | copy-start | bytes 49156
  23.9 16.7 %copy-start.2 = (bf16[32,128]{1,0:T(8,128)(2,1)S(1)}, bf16[32,128]{1,0:T(8,128)(2,1)}, u32[]{:S(2)}) copy-start(bf16[32,128]{1,0:T(8,128)(2,1)} %get-tuple-element.13.sel) | copy-start | bytes 24580
  23.9 19.9 %all-to-all-start.1 = ((bf16[32,4,128]{2,1,0:T(4,128)(2,1)}), bf16[32,4,128]{2,1,0:T(4,128)(2,1)S(1)}, u32[]{:S(2)}, u32[]{:S(2)}) async-start(bf16[32,4,128]{2,1,0:T(4,128)(2,1)} %bitcast.11), calls=%async_computation.1 | async-start | bytes 65536 | tf_op jit(solution)/shard_map/all_to_all | solution.py:232
  40.6 3.2 %copy-start = (bf16[128,128]{1,0:T(8,128)(2,1)S(1)}, bf16[128,128]{1,0:T(8,128)(2,1)}, u32[]{:S(2)}) copy-start(bf16[128,128]{1,0:T(8,128)(2,1)} %w_out.1) | copy-start | bytes 98308

commit v4 on v3

--- a/solution.py
+++ b/solution.py
@@ -14,14 +14,24 @@
 LIMIT = 24 * 1024 * 1024
 HEADS, HD, N = 4, 32, 512
 DEVICES = np.arange(512).reshape(8, 16, 2, 2)
-FAR = 6
-OVER_BLOCK = DEVICES[np.arange(8) ^ FAR].transpose(1, 3, 0, 2).reshape(32, 16).tolist()
-TURN_BIAS, TURN_OUT = 8, 8
-OVER_Z_BIAS = np.roll(DEVICES, -TURN_BIAS, 1).transpose(0, 3, 1, 2).reshape(16, 32).tolist()
-OVER_Z_OUT = np.roll(DEVICES, -TURN_OUT, 1).transpose(0, 3, 1, 2).reshape(16, 32).tolist()
+FAR = [0] + [6] * 15
+OVER_BLOCK = [
+    group
+    for z in range(16)
+    for group in DEVICES[np.arange(8) ^ FAR[z], z].transpose(2, 0, 1).reshape(2, 16).tolist()
+]
+FIRST_BIAS, FIRST_OUT, STEP = 9, 8, 1
+BACK = pow(STEP, -1, 16)
+
+
+def along_z(first):
+    return DEVICES[:, (first + STEP * np.arange(16)) % 16].transpose(0, 3, 1, 2).reshape(16, 32).tolist()
+
+
 OVER_CORE = [[0, 1], [2, 3]]
 Q, I = 32, 16
-MSG = 96
+MSG = 80
+NEAR = 144
 
 
 def nt(a, b):
@@ -41,10 +51,14 @@
     return row // 16, head // 2, head % 2, head
 
 
+def far():
+    return jnp.where(lax.axis_index("row") % 16 == 0, FAR[0], FAR[1])
+
+
 def pack_kernel(
     pair, wq, wk, wv, wg, wb, chain, lists_in, shift_in,
-    out, same_out, sel_out,
-    x, w, wb_v, chain_v, lists, shift, halves, message, same_v, sel_v, sem,
+    out, near_out, same_out, sel_out,
+    x, w, wb_v, chain_v, lists, shift, halves, message, near, same_v, sel_v, sem,
 ):
     b, _, core, head = place()
     copies = [
@@ -69,7 +83,8 @@
     c1 = jnp.where(b1 % 2 == 1, c1, pltpu.roll(c1, 64, 1))
     key_chain = jnp.where(iota((Q, 128), 1) < 64, c0, c1)
     own = jnp.where(b0 == b, 0, 64)
-    sel = iota((Q, 128), 1) == own + (2 * iota((Q, 128), 0) + 4 * TURN_OUT) % 64 + core
+    p = iota((Q, 128), 0)
+    sel = iota((Q, 128), 1) == own + (FIRST_OUT + STEP * (p // 2)) % 16 * 4 + p % 2 * 2 + core
     query_chain = jnp.sum(jnp.where(sel, key_chain, 0.0), axis=-1, keepdims=True)
     same_v[...] = (query_chain == key_chain).astype(F32)
     sel_v[...] = sel.astype(BF16)
@@ -96,52 +111,59 @@
     for c in range(4):
         halves[1, :, c * 128 : (c + 1) * 128] = pltpu.roll(flat[:, c * 128 : (c + 1) * 128].astype(F32), 64, 1).astype(BF16)
     lane = iota((128, 128), 1)
-    for d in range(8):
+
+    def listed(d):
         b0, b1 = lists[0, d], lists[1, d]
         first = halves[b0 % 2, :, pl.ds(pl.multiple_of(b0 // 2 * 128, 128), 128)]
         second = halves[1 - b1 % 2, :, pl.ds(pl.multiple_of(b1 // 2 * 128, 128), 128)]
-        keys = jnp.where(lane < 64, first, second)
-        start = 2 * (d ^ FAR) * MSG
+        return jnp.where(lane < 64, first, second)
+
+    away = far()
+    for n in range(8):
+        keys = listed(n ^ away)
+        start = 2 * n * MSG
         for y in range(2):
             at = start + y * MSG
             message[at : at + 64] = keys[y * 64 : (y + 1) * 64]
             message[at + 64 : at + 80] = w_part
-            message[at + 80 : at + 96] = small
         span = pl.ds(start, 2 * MSG)
-        sent.append(pltpu.make_async_copy(message.at[span], out.at[span], sem.at[11 + d]))
+        sent.append(pltpu.make_async_copy(message.at[span], out.at[span], sem.at[11 + n]))
         sent[-1].start()
+    near[0:128] = listed(b)
+    near[128:144] = small
+    sent.append(pltpu.make_async_copy(near, near_out, sem.at[19]))
+    sent[-1].start()
     for copy in sent:
         copy.wait()
 
 
-def heads_small(g):
-    return sum(g[c, y, 80:96, :].astype(F32) for c in range(2) for y in range(2))
-
-
-def bias_kernel(g, out):
-    b, _, core, _ = place()
-    z = jnp.concatenate(
-        [g[k % 2, 2 * (b ^ FAR) + k // 2, pl.ds(pl.multiple_of(core * 32, 32), 32), :] for k in range(HEADS)], axis=0
-    )
-    found = nn(heads_small(g).astype(BF16), z)[0:4]
+def heads_small(near):
+    return sum(near[k, 128:144, :].astype(F32) for k in range(HEADS))
+
+
+def bias_kernel(near, out):
+    rows = pl.ds(pl.multiple_of(place()[3] * 32, 32), 32)
+    z = jnp.concatenate([near[k, rows, :] for k in range(HEADS)], axis=0)
+    found = nn(heads_small(near).astype(BF16), z)[0:4]
     tile = jnp.concatenate([found] * 4, axis=0).astype(BF16)
     for r in range(8):
         out[r * 16 : (r + 1) * 16, :] = tile
 
 
-def score_kernel(g, same, sel, s_out, v_out, gate_out, zq_scr, k_scr):
-    small = heads_small(g)
+def score_kernel(g, near, same, sel, s_out, v_out, gate_out, zq_scr, k_scr):
+    small = heads_small(near)
     scale = 1.0 / math.sqrt(HD)
     selector = sel[...]
+    away = far()
     w = [
-        jnp.concatenate([g[k % 2, 2 * (s ^ FAR) + k // 2, 64:80, :] for k in range(HEADS) for s in (2 * t, 2 * t + 1)], axis=0)
+        jnp.concatenate([g[k % 2, 2 * (s ^ away) + k // 2, 64:80, :] for k in range(HEADS) for s in (2 * t, 2 * t + 1)], axis=0)
         for t in range(4)
     ]
     w_kv = jnp.concatenate([w[1], w[2]], axis=0)
     w_qg = jnp.concatenate([w[0], w[3]], axis=0)
     for i in range(I):
         s, t = i // 2, i % 2
-        zt = jnp.concatenate([g[k % 2, 2 * (s ^ FAR) + k // 2, t * 32 : (t + 1) * 32, :] for k in range(HEADS)], axis=0)
+        zt = jnp.concatenate([g[k % 2, 2 * s + k // 2, t * 32 : (t + 1) * 32, :] for k in range(HEADS)], axis=0)
         kv = nn(w_kv, zt).astype(BF16)
         k_scr[i] = kv[0:128]
         v_out[i] = kv[128:256]
@@ -161,10 +183,11 @@
 
 def mix_kernel(bias, s_in, v, gate, w_out, out, acc):
     row = iota((128, 128), 0)
-    peer = (row % Q + 2 * (TURN_OUT - TURN_BIAS)) % Q
-    perm = (iota((128, 128), 1) == peer * 4 + row // Q).astype(BF16)
+    n = (row % Q // 2 + BACK * (FIRST_OUT - FIRST_BIAS + 16)) % 16
+    perm = (iota((128, 128), 1) == (2 * n + row % 2) * 4 + row // Q).astype(BF16)
     head_of_lane = iota((Q, 128), 1) // HD
     plane = nn(perm, bias[...])
+    away = far()
     for i in range(I):
         s = s_in[i] + plane
         e = jnp.exp(s - jnp.max(s, axis=-1, keepdims=True))
@@ -173,17 +196,16 @@
         o = every[0:Q]
         for k in range(1, HEADS):
             o = jnp.where(head_of_lane == k, every[k * Q : (k + 1) * Q], o)
-        acc[pl.ds(i, Q, stride=I), :] = jax.nn.sigmoid(gate[i * Q : (i + 1) * Q, :].astype(F32)) * o
+        acc[pl.ds((i // 2 ^ away) * 2 + i % 2, Q, stride=I), :] = jax.nn.sigmoid(gate[i * Q : (i + 1) * Q, :].astype(F32)) * o
     out[...] = nn(acc[...].astype(BF16), w_out[...]).astype(BF16)
 
 
 def order_kernel(moved, out, before, after):
     before[...] = moved[...].astype(F32)
-    for s in range(8):
+    for p in range(32):
+        z = (FIRST_OUT + STEP * (p // 2)) % 16
         for t in range(2):
-            n = 2 * TURN_OUT
-            after[pl.ds(s * 64 + 2 * n + t, 32 - n, stride=2), :] = before[pl.ds(2 * s + t, 32 - n, stride=16), :]
-            after[pl.ds(s * 64 + t, n, stride=2), :] = before[pl.ds((32 - n) * 16 + 2 * s + t, n, stride=16), :]
+            after[pl.ds(4 * z + 2 * (p % 2) + t, 8, stride=64), :] = before[pl.ds(p * 16 + t, 8, stride=2), :]
     out[...] = after[...].astype(BF16)
 
 
@@ -201,11 +223,11 @@
 
 def local(pair, w_query, w_key, w_value, w_gate, w_bias, w_out, shift, block_lists, chain_ids):
     shape = jax.ShapeDtypeStruct
-    packed, same, sel = pl.pallas_call(
+    packed, near, same, sel = pl.pallas_call(
         pack_kernel,
         in_specs=[HBM] * 9,
-        out_specs=[HBM] * 3,
-        out_shape=[shape((16 * MSG, 128), BF16), shape((Q, 128), F32), shape((Q, 128), BF16)],
+        out_specs=[HBM] * 4,
+        out_shape=[shape((16 * MSG, 128), BF16), shape((NEAR, 128), BF16), shape((Q, 128), F32), shape((Q, 128), BF16)],
         scratch_shapes=[
             pltpu.VMEM((4, 32, N), BF16),
             pltpu.VMEM((128, 128), BF16),
@@ -215,9 +237,10 @@
             pltpu.VMEM((1, 1), F32),
             pltpu.VMEM((2, 128, N), BF16),
             pltpu.VMEM((16 * MSG, 128), BF16),
+            pltpu.VMEM((NEAR, 128), BF16),
             pltpu.VMEM((Q, 128), F32),
             pltpu.VMEM((Q, 128), BF16),
-            pltpu.SemaphoreType.DMA((19,)),
+            pltpu.SemaphoreType.DMA((20,)),
         ],
         cost_estimate=pl.CostEstimate(flops=0, bytes_accessed=1000000, transcendentals=0),
     )(
@@ -228,18 +251,19 @@
         packed.reshape(16, MSG, 128), ("row", "head"), 0, 0, tiled=True, axis_index_groups=OVER_BLOCK
     )
     g = lax.all_gather(got, "head", axis=0, axis_index_groups=OVER_CORE)
-    mine = call(bias_kernel, [VMEM], shape((128, 128), BF16), nbytes=400000)(g)
+    near = lax.all_gather(near, "head", axis=0)
+    mine = call(bias_kernel, [VMEM], shape((128, 128), BF16), nbytes=400000)(near)
     bias = lax.all_to_all(
-        mine.reshape(32, 4, 128), ("row", "head"), 0, 0, tiled=True, axis_index_groups=OVER_Z_BIAS
+        mine.reshape(32, 4, 128), ("row", "head"), 0, 0, tiled=True, axis_index_groups=along_z(FIRST_BIAS)
     ).reshape(128, 128)
     scores, v, gate = call(
         score_kernel,
-        [VMEM] * 3,
+        [VMEM] * 4,
         [shape((I, 128, 128), F32), shape((I, 128, 128), BF16), shape((I * Q, 128), BF16)],
         [pltpu.VMEM((I * Q, 128), BF16), pltpu.VMEM((I, 128, 128), BF16)],
         flops=1000000000,
         nbytes=4000000,
-    )(g, same, sel)
+    )(g, near, same, sel)
     mixed = call(
         mix_kernel,
         [VMEM] * 5,
@@ -249,7 +273,7 @@
         nbytes=3000000,
     )(bias, scores, v, gate, w_out)
     moved = lax.all_to_all(
-        mixed.reshape(32, I, 128), ("row", "head"), 0, 0, tiled=True, axis_index_groups=OVER_Z_OUT
+        mixed.reshape(32, I, 128), ("row", "head"), 0, 0, tiled=True, axis_index_groups=along_z(FIRST_OUT)
     ).reshape(512, 128)
     ordered = call(
         order_kernel, [VMEM], shape((512, 128), BF16), [pltpu.VMEM((512, 128), F32)] * 2, nbytes=300000

time: 65 us -> 63.7 us (0.980)
  starting transfers between devices: 16.6 us -> 26 us
  blocking collectives: 39.3 us -> 30.4 us
  waiting for transfers between devices: 2.15 us -> 0.39 us
    all_to_all x1 -> x0, blocking collectives: 13.1 us -> none  [local(): lax.all_to_all(packed.reshape(16, MSG, 128), ('row', 'head'), 0, 0, tiled...]
    all_gather x0 -> x1, blocking collectives: none -> 8.96 us  [local(): near = lax.all_gather(near, 'head', axis=0)]
    all_to_all x0 -> x1, starting transfers between devices: none -> 7.6 us  [local(): lax.all_to_all(packed.reshape(16, MSG, 128), ('row', 'head'), 0, 0, tiled...]
    all_gather x1, blocking collectives: 7.37 us -> 2.63 us  [local(): g = lax.all_gather(got, 'head', axis=0, axis_index_groups=OVER_CORE)]
    all_to_all x1, waiting for transfers between devices: 2.15 us -> 0.38 us  [local(): lax.all_to_all(mine.reshape(32, 4, 128), ('row', 'head'), 0, 0, tiled=Tru...]
    all_to_all x1, starting transfers between devices: 16.6 us -> 18.4 us  [local(): lax.all_to_all(mine.reshape(32, 4, 128), ('row', 'head'), 0, 0, tiled=Tru...]
  transfers between devices with their start and end apart: 1 -> 2, of which waited for: 1 -> 1; matrix products, arithmetic and copies ran while one was open for 0% -> 0% of each run, Pallas kernels for 2% -> 3%
where the time goes in v4:
time: 63.7 us; the launch traced here: 63.3 us
  blocking collectives  30.4 us (48%)
  starting transfers between devices  26 us (41%)
  Pallas kernels  5.75 us (9%)
  between operations  0.73 us (1%)
    all_to_all x1, blocking collectives, local(): lax.all_to_all(mixed.reshape(32, I, 128), ('row', 'head'), 0, 0, tiled=Tr...  18.8 us
    all_to_all x1, starting transfers between devices, local(): lax.all_to_all(mine.reshape(32, 4, 128), ('row', 'head'), 0, 0, tiled=Tru...  18.4 us
    all_gather x1, blocking collectives, local(): near = lax.all_gather(near, 'head', axis=0)  8.96 us
    all_to_all x1, starting transfers between devices, local(): lax.all_to_all(packed.reshape(16, MSG, 128), ('row', 'head'), 0, 0, tiled...  7.6 us
    all_gather x1, blocking collectives, local(): g = lax.all_gather(got, 'head', axis=0, axis_index_groups=OVER_CORE)  2.63 us
    pallas_call x1, Pallas kernels, local(): pl.pallas_call(pack_kernel, in_specs=[HBM] * 9, out_specs=[HBM] * 4, out_...  1.99 us
  transfers between devices with their start and end apart: 2, of which 1 were waited for; matrix products, arithmetic and copies ran while one was open for 0% of the time, Pallas kernels for 3%

profile of v4, /device:TPU:1, one launch (start us, length us, event | category | flops | bytes accessed | tf_op | source)
XLA Modules:
  0.0 63.3 jit_solution(3732454168736723480)
XLA Ops:
  0.7 2.0 %shard_map.100 = (bf16[1280,128]{1,0:T(8,128)(2,1)}, bf16[144,128]{1,0:T(8,128)(2,1)}, f32[32,128]{1,0:T(8,128)}, bf16[32,128]{1,0:T(8,128)(2,1)}) custom-call(bf16[4,32,512]{2,1,0:T(8,128)(2,1)} %bitcast.25, bf16[32,128]{1,0:T(8,128)(2,1)} %bitcast.26, bf16[32,128]{1,0:T(8,128)(2,1)} %bitcast.27, bf16[32,128]{1,0:T(8,128)(2,1)} %bitcast.28, ...), custom_call_target="tpu_custom_call" | custom-call | bytes 1000000 | tf_op jit(solution)/shard_map/pallas_call | solution.py:226
  2.6 0.0 copy-start.3
  2.7 7.6 %all-to-all-start.1 = ((bf16[16,80,128]{2,1,0:T(8,128)(2,1)}), bf16[16,80,128]{2,1,0:T(8,128)(2,1)S(1)}, u32[]{:S(2)}, u32[]{:S(2)}) async-start(bf16[16,80,128]{2,1,0:T(8,128)(2,1)} %bitcast.24), calls=%async_computation.1 | async-start | bytes 655360 | tf_op jit(solution)/shard_map/all_to_all | solution.py:250
  10.3 0.0 copy-done.3
  10.3 9.0 %all-gather = bf16[576,128]{1,0:T(8,128)(2,1)S(1)} all-gather(bf16[144,128]{1,0:T(8,128)(2,1)S(1)} %copy-done.3), channel_id=2, replica_groups=mesh['row'=128,'head'=4] {'head'}, dimensions={0}, use_global_device_ids=true | all-gather | bytes 184320 | tf_op jit(solution)/shard_map/all_gather | solution.py:254
  19.2 0.8 %shard_map.101 = bf16[128,128]{1,0:T(8,128)(2,1)} custom-call(bf16[4,144,128]{2,1,0:T(8,128)(2,1)S(1)} %bitcast.19), custom_call_target="tpu_custom_call" | custom-call | bytes 400000 | tf_op jit(solution)/shard_map/pallas_call | solution.py:255
  20.0 0.0 all-to-all-done.1
  20.0 18.4 %all-to-all-start = ((bf16[32,4,128]{2,1,0:T(4,128)(2,1)}), bf16[32,4,128]{2,1,0:T(4,128)(2,1)S(1)}, u32[]{:S(2)}, u32[]{:S(2)}) async-start(bf16[32,4,128]{2,1,0:T(4,128)(2,1)} %bitcast.10), calls=%async_computation | async-start | bytes 65536 | tf_op jit(solution)/shard_map/all_to_all | solution.py:256
  38.4 0.0 copy-start.1
  38.4 0.0 copy-start.2
  38.4 2.6 %all-gather.1 = bf16[32,80,128]{2,1,0:T(8,128)(2,1)S(1)} all-gather(bf16[16,80,128]{2,1,0:T(8,128)(2,1)S(1)} %all-to-all-done.1), channel_id=3, replica_groups={{0,1},{2,3},{4,5},{6,7},{8,9},{10,11},{12,13},{14,15},{16,17},{18,19},{..., dimensions={0}, use_global_device_ids=true | all-gather | bytes 983040 | tf_op jit(solution)/shard_map/all_gather | solution.py:253
  41.0 0.0 copy-done.1
  41.0 0.0 copy-done.2
  41.0 0.0 copy-start
  41.0 1.0 %shard_map.102 = (f32[16,128,128]{2,1,0:T(8,128)S(1)}, bf16[16,128,128]{2,1,0:T(8,128)(2,1)S(1)}, bf16[512,128]{1,0:T(8,128)(2,1)S(1)}) custom-call(bf16[2,16,80,128]{3,2,1,0:T(8,128)(2,1)S(1)} %bitcast.18, bf16[4,144,128]{2,1,0:T(8,128)(2,1)S(1)} %bitcast.20, f32[32,128]{1,0:T(8,128)S(1)} %copy-done.1, bf16[32,128]{1,0:T(8,128)(2,1)S(1)} %copy-done.2), custom_call_target="tpu_custom_call" | custom-call | flops 1000000000 | bytes 4000000 | tf_op jit(solution)/shard_map/pallas_call | solution.py:259
  42.0 0.4 all-to-all-done
  42.4 0.0 copy-done
  42.4 1.2 %shard_map.103 = bf16[512,128]{1,0:T(8,128)(2,1)S(1)} custom-call(bf16[128,128]{1,0:T(8,128)(2,1)S(1)} %bitcast.23, f32[16,128,128]{2,1,0:T(8,128)S(1)} %get-tuple-element.16.s_in, bf16[16,128,128]{2,1,0:T(8,128)(2,1)S(1)} %get-tuple-element.17.v, bf16[512,128]{1,0:T(8,128)(2,1)S(1)} %get-tuple-element.18.gate, bf16[128,128]{1,0:T(8,128)(2,1)S(1)} %copy-done), custom_call_target="tpu_custom_call" | custom-call | flops 100000000 | bytes 3000000 | tf_op jit(solution)/shard_map/pallas_call | solution.py:267
  43.6 18.8 %all_to_all.15 = bf16[32,16,128]{2,1,0:T(8,128)(2,1)S(1)} all-to-all(bf16[32,16,128]{2,1,0:T(8,128)(2,1)S(1)} %bitcast.22), channel_id=1, replica_groups={{32,34,36,38,40,42,44,46,48,50,52,54,56,58,60,62,0,2,4,6,8,10,12,14,16,..., dimensions={0} | all-to-all | bytes 262144 | tf_op jit(solution)/shard_map/all_to_all | solution.py:275
  62.4 0.8 %shard_map.104 = bf16[512,128]{1,0:T(8,128)(2,1)} custom-call(bf16[512,128]{1,0:T(8,128)(2,1)S(1)} %bitcast.21), custom_call_target="tpu_custom_call" | custom-call | bytes 300000 | tf_op jit(solution)/shard_map/pallas_call | solution.py:278
Async XLA Ops:
  2.6 7.6 %copy-start.3 = (bf16[144,128]{1,0:T(8,128)(2,1)S(1)}, bf16[144,128]{1,0:T(8,128)(2,1)}, u32[]{:S(2)}) copy-start(bf16[144,128]{1,0:T(8,128)(2,1)} %get-tuple-element.12) | copy-start | bytes 110596
  2.7 17.3 %all-to-all-start.1 = ((bf16[16,80,128]{2,1,0:T(8,128)(2,1)}), bf16[16,80,128]{2,1,0:T(8,128)(2,1)S(1)}, u32[]{:S(2)}, u32[]{:S(2)}) async-start(bf16[16,80,128]{2,1,0:T(8,128)(2,1)} %bitcast.24), calls=%async_computation.1 | async-start | bytes 655360 | tf_op jit(solution)/shard_map/all_to_all | solution.py:250
  20.0 22.4 %all-to-all-start = ((bf16[32,4,128]{2,1,0:T(4,128)(2,1)}), bf16[32,4,128]{2,1,0:T(4,128)(2,1)S(1)}, u32[]{:S(2)}, u32[]{:S(2)}) async-start(bf16[32,4,128]{2,1,0:T(4,128)(2,1)} %bitcast.10), calls=%async_computation | async-start | bytes 65536 | tf_op jit(solution)/shard_map/all_to_all | solution.py:256
  38.4 2.7 %copy-start.1 = (f32[32,128]{1,0:T(8,128)S(1)}, f32[32,128]{1,0:T(8,128)}, u32[]{:S(2)}) copy-start(f32[32,128]{1,0:T(8,128)} %get-tuple-element.14.same) | copy-start | bytes 49156
  38.4 2.6 %copy-start.2 = (bf16[32,128]{1,0:T(8,128)(2,1)S(1)}, bf16[32,128]{1,0:T(8,128)(2,1)}, u32[]{:S(2)}) copy-start(bf16[32,128]{1,0:T(8,128)(2,1)} %get-tuple-element.15.sel) | copy-start | bytes 24580
  41.0 1.4 %copy-start = (bf16[128,128]{1,0:T(8,128)(2,1)S(1)}, bf16[128,128]{1,0:T(8,128)(2,1)}, u32[]{:S(2)}) copy-start(bf16[128,128]{1,0:T(8,128)(2,1)} %w_out.1) | copy-start | bytes 98308

commit v5 on v4

--- a/solution.py
+++ b/solution.py
@@ -24,8 +24,9 @@
 BACK = pow(STEP, -1, 16)
 
 
-def along_z(first):
-    return DEVICES[:, (first + STEP * np.arange(16)) % 16].transpose(0, 3, 1, 2).reshape(16, 32).tolist()
+def along_z(first, with_y):
+    order = DEVICES[:, (first + STEP * np.arange(16)) % 16]
+    return (order.transpose(0, 3, 1, 2).reshape(16, 32) if with_y else order.transpose(0, 2, 3, 1).reshape(32, 16)).tolist()
 
 
 OVER_CORE = [[0, 1], [2, 3]]
@@ -142,10 +143,13 @@
 
 
 def bias_kernel(near, out):
-    rows = pl.ds(pl.multiple_of(place()[3] * 32, 32), 32)
-    z = jnp.concatenate([near[k, rows, :] for k in range(HEADS)], axis=0)
-    found = nn(heads_small(near).astype(BF16), z)[0:4]
-    tile = jnp.concatenate([found] * 4, axis=0).astype(BF16)
+    core = place()[2]
+    small = heads_small(near).astype(BF16)
+    found = []
+    for y in range(2):
+        rows = pl.ds(pl.multiple_of((2 * y + core) * 32, 32), 32)
+        found.append(nn(small, jnp.concatenate([near[k, rows, :] for k in range(HEADS)], axis=0))[0:4])
+    tile = jnp.concatenate(found * 2, axis=0).astype(BF16)
     for r in range(8):
         out[r * 16 : (r + 1) * 16, :] = tile
 
@@ -254,7 +258,7 @@
     near = lax.all_gather(near, "head", axis=0)
     mine = call(bias_kernel, [VMEM], shape((128, 128), BF16), nbytes=400000)(near)
     bias = lax.all_to_all(
-        mine.reshape(32, 4, 128), ("row", "head"), 0, 0, tiled=True, axis_index_groups=along_z(FIRST_BIAS)
+        mine.reshape(16, 8, 128), ("row", "head"), 0, 0, tiled=True, axis_index_groups=along_z(FIRST_BIAS, False)
     ).reshape(128, 128)
     scores, v, gate = call(
         score_kernel,
@@ -273,7 +277,7 @@
         nbytes=3000000,
     )(bias, scores, v, gate, w_out)
     moved = lax.all_to_all(
-        mixed.reshape(32, I, 128), ("row", "head"), 0, 0, tiled=True, axis_index_groups=along_z(FIRST_OUT)
+        mixed.reshape(32, I, 128), ("row", "head"), 0, 0, tiled=True, axis_index_groups=along_z(FIRST_OUT, True)
     ).reshape(512, 128)
     ordered = call(
         order_kernel, [VMEM], shape((512, 128), BF16), [pltpu.VMEM((512, 128), F32)] * 2, nbytes=300000

time: 63.7 us -> 62.7 us (0.984)
  starting transfers between devices: 26 us -> 24.3 us
  blocking collectives: 30.4 us -> 31.5 us
    all_to_all x1, starting transfers between devices: 18.4 us -> 16.7 us  [local(): lax.all_to_all(mine.reshape(16, 8, 128), ('row', 'head'), 0, 0, tiled=Tru...]
    all_to_all x1, blocking collectives: 18.8 us -> 19.8 us  [local(): lax.all_to_all(mixed.reshape(32, I, 128), ('row', 'head'), 0, 0, tiled=Tr...]
  transfers between devices with their start and end apart: 2 -> 2, of which waited for: 1 -> 0; matrix products, arithmetic and copies ran while one was open for 0% -> 0% of each run, Pallas kernels for 3% -> 3%
where the time goes in v5:
time: 62.7 us; the launch traced here: 62.3 us
  blocking collectives  31.5 us (50%)
  starting transfers between devices  24.3 us (39%)
  Pallas kernels  5.75 us (9%)
  between operations  0.73 us (1%)
    all_to_all x1, blocking collectives, local(): lax.all_to_all(mixed.reshape(32, I, 128), ('row', 'head'), 0, 0, tiled=Tr...  19.8 us
    all_to_all x1, starting transfers between devices, local(): lax.all_to_all(mine.reshape(16, 8, 128), ('row', 'head'), 0, 0, tiled=Tru...  16.7 us
    all_gather x1, blocking collectives, local(): near = lax.all_gather(near, 'head', axis=0)  8.96 us
    all_to_all x1, starting transfers between devices, local(): lax.all_to_all(packed.reshape(16, MSG, 128), ('row', 'head'), 0, 0, tiled...  7.6 us
    all_gather x1, blocking collectives, local(): g = lax.all_gather(got, 'head', axis=0, axis_index_groups=OVER_CORE)  2.76 us
    pallas_call x1, Pallas kernels, local(): pl.pallas_call(pack_kernel, in_specs=[HBM] * 9, out_specs=[HBM] * 4, out_...  1.99 us
  transfers between devices with their start and end apart: 2, of which 0 were waited for; matrix products, arithmetic and copies ran while one was open for 0% of the time, Pallas kernels for 3%

profile of v5, /device:TPU:1, one launch (start us, length us, event | category | flops | bytes accessed | tf_op | source)
XLA Modules:
  0.0 62.3 jit_solution(15869892230917705085)
XLA Ops:
  0.7 2.0 %shard_map.100 = (bf16[1280,128]{1,0:T(8,128)(2,1)}, bf16[144,128]{1,0:T(8,128)(2,1)}, f32[32,128]{1,0:T(8,128)}, bf16[32,128]{1,0:T(8,128)(2,1)}) custom-call(bf16[4,32,512]{2,1,0:T(8,128)(2,1)} %bitcast.25, bf16[32,128]{1,0:T(8,128)(2,1)} %bitcast.26, bf16[32,128]{1,0:T(8,128)(2,1)} %bitcast.27, bf16[32,128]{1,0:T(8,128)(2,1)} %bitcast.28, ...), custom_call_target="tpu_custom_call" | custom-call | bytes 1000000 | tf_op jit(solution)/shard_map/pallas_call | solution.py:230
  2.6 0.0 copy-start.3
  2.7 7.6 %all-to-all-start.1 = ((bf16[16,80,128]{2,1,0:T(8,128)(2,1)}), bf16[16,80,128]{2,1,0:T(8,128)(2,1)S(1)}, u32[]{:S(2)}, u32[]{:S(2)}) async-start(bf16[16,80,128]{2,1,0:T(8,128)(2,1)} %bitcast.24), calls=%async_computation.1 | async-start | bytes 655360 | tf_op jit(solution)/shard_map/all_to_all | solution.py:254
  10.3 0.0 copy-done.3
  10.3 9.0 %all-gather = bf16[576,128]{1,0:T(8,128)(2,1)S(1)} all-gather(bf16[144,128]{1,0:T(8,128)(2,1)S(1)} %copy-done.3), channel_id=2, replica_groups=mesh['row'=128,'head'=4] {'head'}, dimensions={0}, use_global_device_ids=true | all-gather | bytes 184320 | tf_op jit(solution)/shard_map/all_gather | solution.py:258
  19.2 0.8 %shard_map.101 = bf16[128,128]{1,0:T(8,128)(2,1)} custom-call(bf16[4,144,128]{2,1,0:T(8,128)(2,1)S(1)} %bitcast.19), custom_call_target="tpu_custom_call" | custom-call | bytes 400000 | tf_op jit(solution)/shard_map/pallas_call | solution.py:259
  20.0 0.0 all-to-all-done.1
  20.0 16.7 %all-to-all-start = ((bf16[16,8,128]{2,1,0:T(8,128)(2,1)}), bf16[16,8,128]{2,1,0:T(8,128)(2,1)S(1)}, u32[]{:S(2)}, u32[]{:S(2)}) async-start(bf16[16,8,128]{2,1,0:T(8,128)(2,1)} %bitcast.10), calls=%async_computation | async-start | bytes 65536 | tf_op jit(solution)/shard_map/all_to_all | solution.py:260
  36.7 0.0 copy-start.1
  36.7 0.0 copy-start.2
  36.7 2.8 %all-gather.1 = bf16[32,80,128]{2,1,0:T(8,128)(2,1)S(1)} all-gather(bf16[16,80,128]{2,1,0:T(8,128)(2,1)S(1)} %all-to-all-done.1), channel_id=3, replica_groups={{0,1},{2,3},{4,5},{6,7},{8,9},{10,11},{12,13},{14,15},{16,17},{18,19},{..., dimensions={0}, use_global_device_ids=true | all-gather | bytes 983040 | tf_op jit(solution)/shard_map/all_gather | solution.py:257
  39.5 0.0 copy-done.1
  39.5 0.0 copy-done.2
  39.5 0.0 copy-start
  39.5 1.0 %shard_map.102 = (f32[16,128,128]{2,1,0:T(8,128)S(1)}, bf16[16,128,128]{2,1,0:T(8,128)(2,1)S(1)}, bf16[512,128]{1,0:T(8,128)(2,1)S(1)}) custom-call(bf16[2,16,80,128]{3,2,1,0:T(8,128)(2,1)S(1)} %bitcast.18, bf16[4,144,128]{2,1,0:T(8,128)(2,1)S(1)} %bitcast.20, f32[32,128]{1,0:T(8,128)S(1)} %copy-done.1, bf16[32,128]{1,0:T(8,128)(2,1)S(1)} %copy-done.2), custom_call_target="tpu_custom_call" | custom-call | flops 1000000000 | bytes 4000000 | tf_op jit(solution)/shard_map/pallas_call | solution.py:263
  40.5 0.0 all-to-all-done
  40.5 0.0 copy-done
  40.5 1.2 %shard_map.103 = bf16[512,128]{1,0:T(8,128)(2,1)S(1)} custom-call(bf16[128,128]{1,0:T(8,128)(2,1)S(1)} %bitcast.23, f32[16,128,128]{2,1,0:T(8,128)S(1)} %get-tuple-element.16.s_in, bf16[16,128,128]{2,1,0:T(8,128)(2,1)S(1)} %get-tuple-element.17.v, bf16[512,128]{1,0:T(8,128)(2,1)S(1)} %get-tuple-element.18.gate, bf16[128,128]{1,0:T(8,128)(2,1)S(1)} %copy-done), custom_call_target="tpu_custom_call" | custom-call | flops 100000000 | bytes 3000000 | tf_op jit(solution)/shard_map/pallas_call | solution.py:271
  41.7 19.8 %all_to_all.15 = bf16[32,16,128]{2,1,0:T(8,128)(2,1)S(1)} all-to-all(bf16[32,16,128]{2,1,0:T(8,128)(2,1)S(1)} %bitcast.22), channel_id=1, replica_groups={{32,34,36,38,40,42,44,46,48,50,52,54,56,58,60,62,0,2,4,6,8,10,12,14,16,..., dimensions={0} | all-to-all | bytes 262144 | tf_op jit(solution)/shard_map/all_to_all | solution.py:279
  61.5 0.8 %shard_map.104 = bf16[512,128]{1,0:T(8,128)(2,1)} custom-call(bf16[512,128]{1,0:T(8,128)(2,1)S(1)} %bitcast.21), custom_call_target="tpu_custom_call" | custom-call | bytes 300000 | tf_op jit(solution)/shard_map/pallas_call | solution.py:282
Async XLA Ops:
  2.6 7.6 %copy-start.3 = (bf16[144,128]{1,0:T(8,128)(2,1)S(1)}, bf16[144,128]{1,0:T(8,128)(2,1)}, u32[]{:S(2)}) copy-start(bf16[144,128]{1,0:T(8,128)(2,1)} %get-tuple-element.12) | copy-start | bytes 110596
  2.7 17.3 %all-to-all-start.1 = ((bf16[16,80,128]{2,1,0:T(8,128)(2,1)}), bf16[16,80,128]{2,1,0:T(8,128)(2,1)S(1)}, u32[]{:S(2)}, u32[]{:S(2)}) async-start(bf16[16,80,128]{2,1,0:T(8,128)(2,1)} %bitcast.24), calls=%async_computation.1 | async-start | bytes 655360 | tf_op jit(solution)/shard_map/all_to_all | solution.py:254
  20.0 20.5 %all-to-all-start = ((bf16[16,8,128]{2,1,0:T(8,128)(2,1)}), bf16[16,8,128]{2,1,0:T(8,128)(2,1)S(1)}, u32[]{:S(2)}, u32[]{:S(2)}) async-start(bf16[16,8,128]{2,1,0:T(8,128)(2,1)} %bitcast.10), calls=%async_computation | async-start | bytes 65536 | tf_op jit(solution)/shard_map/all_to_all | solution.py:260
  36.7 2.8 %copy-start.1 = (f32[32,128]{1,0:T(8,128)S(1)}, f32[32,128]{1,0:T(8,128)}, u32[]{:S(2)}) copy-start(f32[32,128]{1,0:T(8,128)} %get-tuple-element.14.same) | copy-start | bytes 49156
  36.7 2.8 %copy-start.2 = (bf16[32,128]{1,0:T(8,128)(2,1)S(1)}, bf16[32,128]{1,0:T(8,128)(2,1)}, u32[]{:S(2)}) copy-start(bf16[32,128]{1,0:T(8,128)(2,1)} %get-tuple-element.15.sel) | copy-start | bytes 24580
  39.5 1.0 %copy-start = (bf16[128,128]{1,0:T(8,128)(2,1)S(1)}, bf16[128,128]{1,0:T(8,128)(2,1)}, u32[]{:S(2)}) copy-start(bf16[128,128]{1,0:T(8,128)(2,1)} %w_out.1) | copy-start | bytes 98308

commit v6 on v5

--- a/solution.py
+++ b/solution.py
@@ -20,12 +20,11 @@
     for z in range(16)
     for group in DEVICES[np.arange(8) ^ FAR[z], z].transpose(2, 0, 1).reshape(2, 16).tolist()
 ]
-FIRST_BIAS, FIRST_OUT, STEP = 9, 8, 1
-BACK = pow(STEP, -1, 16)
+FIRST_BIAS, FIRST_OUT = 11, 8
 
 
 def along_z(first, with_y):
-    order = DEVICES[:, (first + STEP * np.arange(16)) % 16]
+    order = DEVICES[:, (first + np.arange(16)) % 16]
     return (order.transpose(0, 3, 1, 2).reshape(16, 32) if with_y else order.transpose(0, 2, 3, 1).reshape(32, 16)).tolist()
 
 
@@ -85,7 +84,7 @@
     key_chain = jnp.where(iota((Q, 128), 1) < 64, c0, c1)
     own = jnp.where(b0 == b, 0, 64)
     p = iota((Q, 128), 0)
-    sel = iota((Q, 128), 1) == own + (FIRST_OUT + STEP * (p // 2)) % 16 * 4 + p % 2 * 2 + core
+    sel = iota((Q, 128), 1) == own + (FIRST_OUT + p // 2) % 16 * 4 + p % 2 * 2 + core
     query_chain = jnp.sum(jnp.where(sel, key_chain, 0.0), axis=-1, keepdims=True)
     same_v[...] = (query_chain == key_chain).astype(F32)
     sel_v[...] = sel.astype(BF16)
@@ -119,6 +118,10 @@
         second = halves[1 - b1 % 2, :, pl.ds(pl.multiple_of(b1 // 2 * 128, 128), 128)]
         return jnp.where(lane < 64, first, second)
 
+    near[0:128] = listed(b)
+    near[128:144] = small
+    sent.append(pltpu.make_async_copy(near, near_out, sem.at[19]))
+    sent[-1].start()
     away = far()
     for n in range(8):
         keys = listed(n ^ away)
@@ -130,10 +133,6 @@
         span = pl.ds(start, 2 * MSG)
         sent.append(pltpu.make_async_copy(message.at[span], out.at[span], sem.at[11 + n]))
         sent[-1].start()
-    near[0:128] = listed(b)
-    near[128:144] = small
-    sent.append(pltpu.make_async_copy(near, near_out, sem.at[19]))
-    sent[-1].start()
     for copy in sent:
         copy.wait()
 
@@ -187,7 +186,7 @@
 
 def mix_kernel(bias, s_in, v, gate, w_out, out, acc):
     row = iota((128, 128), 0)
-    n = (row % Q // 2 + BACK * (FIRST_OUT - FIRST_BIAS + 16)) % 16
+    n = (row % Q // 2 + FIRST_OUT - FIRST_BIAS + 16) % 16
     perm = (iota((128, 128), 1) == (2 * n + row % 2) * 4 + row // Q).astype(BF16)
     head_of_lane = iota((Q, 128), 1) // HD
     plane = nn(perm, bias[...])
@@ -204,13 +203,20 @@
     out[...] = nn(acc[...].astype(BF16), w_out[...]).astype(BF16)
 
 
-def order_kernel(moved, out, before, after):
+def order_kernel(moved, out, before, after, stage, sem):
     before[...] = moved[...].astype(F32)
-    for p in range(32):
-        z = (FIRST_OUT + STEP * (p // 2)) % 16
+    turn, left = 2 * FIRST_OUT, 32 - 2 * FIRST_OUT
+    copies = []
+    for s in range(8):
         for t in range(2):
-            after[pl.ds(4 * z + 2 * (p % 2) + t, 8, stride=64), :] = before[pl.ds(p * 16 + t, 8, stride=2), :]
-    out[...] = after[...].astype(BF16)
+            after[pl.ds(s * 64 + 2 * turn + t, left, stride=2), :] = before[pl.ds(2 * s + t, left, stride=16), :]
+            after[pl.ds(s * 64 + t, turn, stride=2), :] = before[pl.ds(left * 16 + 2 * s + t, turn, stride=16), :]
+        span = pl.ds(s * 64, 64)
+        stage[span, :] = after[span, :].astype(BF16)
+        copies.append(pltpu.make_async_copy(stage.at[span], out.at[span], sem.at[s]))
+        copies[-1].start()
+    for copy in copies:
+        copy.wait()
 
 
 def call(kernel, ins, outs, scratch=(), flops=0, nbytes=0):
@@ -279,8 +285,19 @@
     moved = lax.all_to_all(
         mixed.reshape(32, I, 128), ("row", "head"), 0, 0, tiled=True, axis_index_groups=along_z(FIRST_OUT, True)
     ).reshape(512, 128)
-    ordered = call(
-        order_kernel, [VMEM], shape((512, 128), BF16), [pltpu.VMEM((512, 128), F32)] * 2, nbytes=300000
+    ordered = pl.pallas_call(
+        order_kernel,
+        in_specs=[VMEM],
+        out_specs=HBM,
+        out_shape=shape((512, 128), BF16),
+        scratch_shapes=[
+            pltpu.VMEM((512, 128), F32),
+            pltpu.VMEM((512, 128), F32),
+            pltpu.VMEM((512, 128), BF16),
+            pltpu.SemaphoreType.DMA((8,)),
+        ],
+        compiler_params=pltpu.CompilerParams(vmem_limit_bytes=LIMIT),
+        cost_estimate=pl.CostEstimate(flops=0, bytes_accessed=300000, transcendentals=0),
     )(moved)
     return ordered.reshape(512, 1, 128)
 

time: 62.7 us -> 62 us (0.989)
  starting transfers between devices: 24.3 us -> 22.5 us
  waiting for transfers between devices: 0.01 us -> 1.29 us
    all_to_all x1, starting transfers between devices: 16.7 us -> 14.9 us  [local(): lax.all_to_all(mine.reshape(16, 8, 128), ('row', 'head'), 0, 0, tiled=Tru...]
    all_to_all x1, waiting for transfers between devices: 0.01 us -> 1.28 us  [local(): lax.all_to_all(mine.reshape(16, 8, 128), ('row', 'head'), 0, 0, tiled=Tru...]
  transfers between devices with their start and end apart: 2 -> 2, of which waited for: 0 -> 1; matrix products, arithmetic and copies ran while one was open for 0% -> 0% of each run, Pallas kernels for 3% -> 3%
where the time goes in v6:
time: 62 us; the launch traced here: 61.6 us
  blocking collectives  31.3 us (50%)
  starting transfers between devices  22.5 us (36%)
  Pallas kernels  5.76 us (9%)
  waiting for transfers between devices  1.29 us (2%)
  between operations  0.72 us (1%)
    all_to_all x1, blocking collectives, local(): lax.all_to_all(mixed.reshape(32, I, 128), ('row', 'head'), 0, 0, tiled=Tr...  19.6 us
    all_to_all x1, starting transfers between devices, local(): lax.all_to_all(mine.reshape(16, 8, 128), ('row', 'head'), 0, 0, tiled=Tru...  14.9 us
    all_gather x1, blocking collectives, local(): near = lax.all_gather(near, 'head', axis=0)  8.96 us
    all_to_all x1, starting transfers between devices, local(): lax.all_to_all(packed.reshape(16, MSG, 128), ('row', 'head'), 0, 0, tiled...  7.6 us
    all_gather x1, blocking collectives, local(): g = lax.all_gather(got, 'head', axis=0, axis_index_groups=OVER_CORE)  2.76 us
    pallas_call x1, Pallas kernels, local(): pl.pallas_call(pack_kernel, in_specs=[HBM] * 9, out_specs=[HBM] * 4, out_...  1.99 us
    all_to_all x1, waiting for transfers between devices, local(): lax.all_to_all(mine.reshape(16, 8, 128), ('row', 'head'), 0, 0, tiled=Tru...  1.28 us
  transfers between devices with their start and end apart: 2, of which 1 were waited for; matrix products, arithmetic and copies ran while one was open for 0% of the time, Pallas kernels for 3%

profile of v6, /device:TPU:1, one launch (start us, length us, event | category | flops | bytes accessed | tf_op | source)
XLA Modules:
  0.0 61.6 jit_solution(8120552737680920428)
XLA Ops:
  0.7 2.0 %shard_map.100 = (bf16[1280,128]{1,0:T(8,128)(2,1)}, bf16[144,128]{1,0:T(8,128)(2,1)}, f32[32,128]{1,0:T(8,128)}, bf16[32,128]{1,0:T(8,128)(2,1)}) custom-call(bf16[4,32,512]{2,1,0:T(8,128)(2,1)} %bitcast.25, bf16[32,128]{1,0:T(8,128)(2,1)} %bitcast.26, bf16[32,128]{1,0:T(8,128)(2,1)} %bitcast.27, bf16[32,128]{1,0:T(8,128)(2,1)} %bitcast.28, ...), custom_call_target="tpu_custom_call" | custom-call | bytes 1000000 | tf_op jit(solution)/shard_map/pallas_call | solution.py:236
  2.7 0.0 copy-start.3
  2.7 7.6 %all-to-all-start.1 = ((bf16[16,80,128]{2,1,0:T(8,128)(2,1)}), bf16[16,80,128]{2,1,0:T(8,128)(2,1)S(1)}, u32[]{:S(2)}, u32[]{:S(2)}) async-start(bf16[16,80,128]{2,1,0:T(8,128)(2,1)} %bitcast.24), calls=%async_computation.1 | async-start | bytes 655360 | tf_op jit(solution)/shard_map/all_to_all | solution.py:260
  10.3 0.0 copy-done.3
  10.3 9.0 %all-gather = bf16[576,128]{1,0:T(8,128)(2,1)S(1)} all-gather(bf16[144,128]{1,0:T(8,128)(2,1)S(1)} %copy-done.3), channel_id=2, replica_groups=mesh['row'=128,'head'=4] {'head'}, dimensions={0}, use_global_device_ids=true | all-gather | bytes 184320 | tf_op jit(solution)/shard_map/all_gather | solution.py:264
  19.2 0.8 %shard_map.101 = bf16[128,128]{1,0:T(8,128)(2,1)} custom-call(bf16[4,144,128]{2,1,0:T(8,128)(2,1)S(1)} %bitcast.19), custom_call_target="tpu_custom_call" | custom-call | bytes 400000 | tf_op jit(solution)/shard_map/pallas_call | solution.py:265
  20.0 0.0 all-to-all-done.1
  20.0 14.9 %all-to-all-start = ((bf16[16,8,128]{2,1,0:T(8,128)(2,1)}), bf16[16,8,128]{2,1,0:T(8,128)(2,1)S(1)}, u32[]{:S(2)}, u32[]{:S(2)}) async-start(bf16[16,8,128]{2,1,0:T(8,128)(2,1)} %bitcast.10), calls=%async_computation | async-start | bytes 65536 | tf_op jit(solution)/shard_map/all_to_all | solution.py:266
  34.9 0.0 copy-start.1
  34.9 0.0 copy-start.2
  34.9 2.8 %all-gather.1 = bf16[32,80,128]{2,1,0:T(8,128)(2,1)S(1)} all-gather(bf16[16,80,128]{2,1,0:T(8,128)(2,1)S(1)} %all-to-all-done.1), channel_id=3, replica_groups={{0,1},{2,3},{4,5},{6,7},{8,9},{10,11},{12,13},{14,15},{16,17},{18,19},{..., dimensions={0}, use_global_device_ids=true | all-gather | bytes 983040 | tf_op jit(solution)/shard_map/all_gather | solution.py:263
  37.7 0.0 copy-done.1
  37.7 0.0 copy-done.2
  37.7 0.0 copy-start
  37.7 1.0 %shard_map.102 = (f32[16,128,128]{2,1,0:T(8,128)S(1)}, bf16[16,128,128]{2,1,0:T(8,128)(2,1)S(1)}, bf16[512,128]{1,0:T(8,128)(2,1)S(1)}) custom-call(bf16[2,16,80,128]{3,2,1,0:T(8,128)(2,1)S(1)} %bitcast.18, bf16[4,144,128]{2,1,0:T(8,128)(2,1)S(1)} %bitcast.20, f32[32,128]{1,0:T(8,128)S(1)} %copy-done.1, bf16[32,128]{1,0:T(8,128)(2,1)S(1)} %copy-done.2), custom_call_target="tpu_custom_call" | custom-call | flops 1000000000 | bytes 4000000 | tf_op jit(solution)/shard_map/pallas_call | solution.py:269
  38.7 1.3 %all-to-all-done = bf16[16,8,128]{2,1,0:T(8,128)(2,1)S(1)} async-done(((bf16[16,8,128]{2,1,0:T(8,128)(2,1)}), bf16[16,8,128]{2,1,0:T(8,128)(2,1)S(1)}, u32[]{:S(2)}, u32[]{:S(2)}) %all-to-all-start) | async-done | bytes 32800 | tf_op jit(solution)/shard_map/all_to_all | solution.py:266
  40.0 0.0 copy-done
  40.0 1.2 %shard_map.103 = bf16[512,128]{1,0:T(8,128)(2,1)S(1)} custom-call(bf16[128,128]{1,0:T(8,128)(2,1)S(1)} %bitcast.23, f32[16,128,128]{2,1,0:T(8,128)S(1)} %get-tuple-element.16.s_in, bf16[16,128,128]{2,1,0:T(8,128)(2,1)S(1)} %get-tuple-element.17.v, bf16[512,128]{1,0:T(8,128)(2,1)S(1)} %get-tuple-element.18.gate, bf16[128,128]{1,0:T(8,128)(2,1)S(1)} %copy-done), custom_call_target="tpu_custom_call" | custom-call | flops 100000000 | bytes 3000000 | tf_op jit(solution)/shard_map/pallas_call | solution.py:277
  41.2 19.6 %all_to_all.15 = bf16[32,16,128]{2,1,0:T(8,128)(2,1)S(1)} all-to-all(bf16[32,16,128]{2,1,0:T(8,128)(2,1)S(1)} %bitcast.22), channel_id=1, replica_groups={{32,34,36,38,40,42,44,46,48,50,52,54,56,58,60,62,0,2,4,6,8,10,12,14,16,..., dimensions={0} | all-to-all | bytes 262144 | tf_op jit(solution)/shard_map/all_to_all | solution.py:285
  60.8 0.8 %shard_map.104 = bf16[512,128]{1,0:T(8,128)(2,1)} custom-call(bf16[512,128]{1,0:T(8,128)(2,1)S(1)} %bitcast.21), custom_call_target="tpu_custom_call" | custom-call | bytes 300000 | tf_op jit(solution)/shard_map/pallas_call | solution.py:288
Async XLA Ops:
  2.7 7.6 %copy-start.3 = (bf16[144,128]{1,0:T(8,128)(2,1)S(1)}, bf16[144,128]{1,0:T(8,128)(2,1)}, u32[]{:S(2)}) copy-start(bf16[144,128]{1,0:T(8,128)(2,1)} %get-tuple-element.12) | copy-start | bytes 110596
  2.7 17.3 %all-to-all-start.1 = ((bf16[16,80,128]{2,1,0:T(8,128)(2,1)}), bf16[16,80,128]{2,1,0:T(8,128)(2,1)S(1)}, u32[]{:S(2)}, u32[]{:S(2)}) async-start(bf16[16,80,128]{2,1,0:T(8,128)(2,1)} %bitcast.24), calls=%async_computation.1 | async-start | bytes 655360 | tf_op jit(solution)/shard_map/all_to_all | solution.py:260
  20.0 20.0 %all-to-all-start = ((bf16[16,8,128]{2,1,0:T(8,128)(2,1)}), bf16[16,8,128]{2,1,0:T(8,128)(2,1)S(1)}, u32[]{:S(2)}, u32[]{:S(2)}) async-start(bf16[16,8,128]{2,1,0:T(8,128)(2,1)} %bitcast.10), calls=%async_computation | async-start | bytes 65536 | tf_op jit(solution)/shard_map/all_to_all | solution.py:266
  34.9 2.8 %copy-start.1 = (f32[32,128]{1,0:T(8,128)S(1)}, f32[32,128]{1,0:T(8,128)}, u32[]{:S(2)}) copy-start(f32[32,128]{1,0:T(8,128)} %get-tuple-element.14.same) | copy-start | bytes 49156
  34.9 2.8 %copy-start.2 = (bf16[32,128]{1,0:T(8,128)(2,1)S(1)}, bf16[32,128]{1,0:T(8,128)(2,1)}, u32[]{:S(2)}) copy-start(bf16[32,128]{1,0:T(8,128)(2,1)} %get-tuple-element.15.sel) | copy-start | bytes 24580
  37.7 2.3 %copy-start = (bf16[128,128]{1,0:T(8,128)(2,1)S(1)}, bf16[128,128]{1,0:T(8,128)(2,1)}, u32[]{:S(2)}) copy-start(bf16[128,128]{1,0:T(8,128)(2,1)} %w_out.1) | copy-start | bytes 98308

commit v7 on v6

--- a/solution.py
+++ b/solution.py
@@ -153,7 +153,7 @@
         out[r * 16 : (r + 1) * 16, :] = tile
 
 
-def score_kernel(g, near, same, sel, s_out, v_out, gate_out, zq_scr, k_scr):
+def score_kernel(g, near, same, sel, s_out, v_out, gate_out, moved_out, zq_scr, k_scr):
     small = heads_small(near)
     scale = 1.0 / math.sqrt(HD)
     selector = sel[...]
@@ -174,25 +174,25 @@
     qg = nt(zq_scr[...], w_qg).astype(BF16)
     gate_out[...] = qg[:, 128:256]
     head_of_lane = iota((Q, 128), 1) // HD
-    moved = jnp.concatenate(
+    moved_out[...] = jnp.concatenate(
         [same[...] * (small[4 + k : 5 + k] + small[8 + k : 9 + k] + small[12 + k : 13 + k]) for k in range(HEADS)], axis=0
     )
     for i in range(I):
         q = qg[i * Q : (i + 1) * Q, 0:128]
         zero = jnp.zeros_like(q)
         q_all = jnp.concatenate([jnp.where(head_of_lane == k, q, zero) for k in range(HEADS)], axis=0)
-        s_out[i] = nn(q_all, k_scr[i]) * scale + moved
-
-
-def mix_kernel(bias, s_in, v, gate, w_out, out, acc):
+        s_out[i] = nn(q_all, k_scr[i]) * scale
+
+
+def mix_kernel(bias, s_in, v, gate, moved, w_out, out, acc):
     row = iota((128, 128), 0)
     n = (row % Q // 2 + FIRST_OUT - FIRST_BIAS + 16) % 16
     perm = (iota((128, 128), 1) == (2 * n + row % 2) * 4 + row // Q).astype(BF16)
     head_of_lane = iota((Q, 128), 1) // HD
-    plane = nn(perm, bias[...])
+    logit_bias = nn(perm, bias[...]) + moved[...]
     away = far()
     for i in range(I):
-        s = s_in[i] + plane
+        s = s_in[i] + logit_bias
         e = jnp.exp(s - jnp.max(s, axis=-1, keepdims=True))
         p = (e * (1.0 / jnp.sum(e, axis=-1, keepdims=True))).astype(BF16)
         every = nt(p, v[i])
@@ -266,23 +266,23 @@
     bias = lax.all_to_all(
         mine.reshape(16, 8, 128), ("row", "head"), 0, 0, tiled=True, axis_index_groups=along_z(FIRST_BIAS, False)
     ).reshape(128, 128)
-    scores, v, gate = call(
+    scores, v, gate, moved = call(
         score_kernel,
         [VMEM] * 4,
-        [shape((I, 128, 128), F32), shape((I, 128, 128), BF16), shape((I * Q, 128), BF16)],
+        [shape((I, 128, 128), F32), shape((I, 128, 128), BF16), shape((I * Q, 128), BF16), shape((128, 128), F32)],
         [pltpu.VMEM((I * Q, 128), BF16), pltpu.VMEM((I, 128, 128), BF16)],
         flops=1000000000,
         nbytes=4000000,
     )(g, near, same, sel)
     mixed = call(
         mix_kernel,
-        [VMEM] * 5,
+        [VMEM] * 6,
         shape((I * Q, 128), BF16),
         [pltpu.VMEM((I * Q, 128), F32)],
         flops=100000000,
         nbytes=3000000,
-    )(bias, scores, v, gate, w_out)
-    moved = lax.all_to_all(
+    )(bias, scores, v, gate, moved, w_out)
+    arrived = lax.all_to_all(
         mixed.reshape(32, I, 128), ("row", "head"), 0, 0, tiled=True, axis_index_groups=along_z(FIRST_OUT, True)
     ).reshape(512, 128)
     ordered = pl.pallas_call(
@@ -298,7 +298,7 @@
         ],
         compiler_params=pltpu.CompilerParams(vmem_limit_bytes=LIMIT),
         cost_estimate=pl.CostEstimate(flops=0, bytes_accessed=300000, transcendentals=0),
-    )(moved)
+    )(arrived)
     return ordered.reshape(512, 1, 128)
 
 

time: 62 us -> 62 us (level)
  no operation moved by 1% of the time
where the time goes in v7:
time: 62 us; the launch traced here: 61.6 us
  blocking collectives  31.3 us (50%)
  starting transfers between devices  22.5 us (36%)
  Pallas kernels  5.76 us (9%)
  waiting for transfers between devices  1.29 us (2%)
  between operations  0.71 us (1%)
    all_to_all x1, blocking collectives, local(): lax.all_to_all(mixed.reshape(32, I, 128), ('row', 'head'), 0, 0, tiled=Tr...  19.6 us
    all_to_all x1, starting transfers between devices, local(): lax.all_to_all(mine.reshape(16, 8, 128), ('row', 'head'), 0, 0, tiled=Tru...  14.9 us
    all_gather x1, blocking collectives, local(): near = lax.all_gather(near, 'head', axis=0)  8.96 us
    all_to_all x1, starting transfers between devices, local(): lax.all_to_all(packed.reshape(16, MSG, 128), ('row', 'head'), 0, 0, tiled...  7.6 us
    all_gather x1, blocking collectives, local(): g = lax.all_gather(got, 'head', axis=0, axis_index_groups=OVER_CORE)  2.76 us
    pallas_call x1, Pallas kernels, local(): pl.pallas_call(pack_kernel, in_specs=[HBM] * 9, out_specs=[HBM] * 4, out_...  1.99 us
    all_to_all x1, waiting for transfers between devices, local(): lax.all_to_all(mine.reshape(16, 8, 128), ('row', 'head'), 0, 0, tiled=Tru...  1.29 us
  transfers between devices with their start and end apart: 2, of which 1 were waited for; matrix products, arithmetic and copies ran while one was open for 0% of the time, Pallas kernels for 3%

profile of v7, /device:TPU:1, one launch (start us, length us, event | category | flops | bytes accessed | tf_op | source)
XLA Modules:
  0.0 61.6 jit_solution(14545962154774147301)
XLA Ops:
  0.7 2.0 %shard_map.100 = (bf16[1280,128]{1,0:T(8,128)(2,1)}, bf16[144,128]{1,0:T(8,128)(2,1)}, f32[32,128]{1,0:T(8,128)}, bf16[32,128]{1,0:T(8,128)(2,1)}) custom-call(bf16[4,32,512]{2,1,0:T(8,128)(2,1)} %bitcast.25, bf16[32,128]{1,0:T(8,128)(2,1)} %bitcast.26, bf16[32,128]{1,0:T(8,128)(2,1)} %bitcast.27, bf16[32,128]{1,0:T(8,128)(2,1)} %bitcast.28, ...), custom_call_target="tpu_custom_call" | custom-call | bytes 1000000 | tf_op jit(solution)/shard_map/pallas_call | solution.py:236
  2.7 0.0 copy-start.3
  2.7 7.6 %all-to-all-start.1 = ((bf16[16,80,128]{2,1,0:T(8,128)(2,1)}), bf16[16,80,128]{2,1,0:T(8,128)(2,1)S(1)}, u32[]{:S(2)}, u32[]{:S(2)}) async-start(bf16[16,80,128]{2,1,0:T(8,128)(2,1)} %bitcast.24), calls=%async_computation.1 | async-start | bytes 655360 | tf_op jit(solution)/shard_map/all_to_all | solution.py:260
  10.3 0.0 copy-done.3
  10.3 9.0 %all-gather = bf16[576,128]{1,0:T(8,128)(2,1)S(1)} all-gather(bf16[144,128]{1,0:T(8,128)(2,1)S(1)} %copy-done.3), channel_id=2, replica_groups=mesh['row'=128,'head'=4] {'head'}, dimensions={0}, use_global_device_ids=true | all-gather | bytes 184320 | tf_op jit(solution)/shard_map/all_gather | solution.py:264
  19.2 0.8 %shard_map.101 = bf16[128,128]{1,0:T(8,128)(2,1)} custom-call(bf16[4,144,128]{2,1,0:T(8,128)(2,1)S(1)} %bitcast.19), custom_call_target="tpu_custom_call" | custom-call | bytes 400000 | tf_op jit(solution)/shard_map/pallas_call | solution.py:265
  20.0 0.0 all-to-all-done.1
  20.0 14.9 %all-to-all-start = ((bf16[16,8,128]{2,1,0:T(8,128)(2,1)}), bf16[16,8,128]{2,1,0:T(8,128)(2,1)S(1)}, u32[]{:S(2)}, u32[]{:S(2)}) async-start(bf16[16,8,128]{2,1,0:T(8,128)(2,1)} %bitcast.10), calls=%async_computation | async-start | bytes 65536 | tf_op jit(solution)/shard_map/all_to_all | solution.py:266
  34.9 0.0 copy-start.1
  34.9 0.0 copy-start.2
  34.9 2.8 %all-gather.1 = bf16[32,80,128]{2,1,0:T(8,128)(2,1)S(1)} all-gather(bf16[16,80,128]{2,1,0:T(8,128)(2,1)S(1)} %all-to-all-done.1), channel_id=3, replica_groups={{0,1},{2,3},{4,5},{6,7},{8,9},{10,11},{12,13},{14,15},{16,17},{18,19},{..., dimensions={0}, use_global_device_ids=true | all-gather | bytes 983040 | tf_op jit(solution)/shard_map/all_gather | solution.py:263
  37.7 0.0 copy-done.1
  37.7 0.0 copy-done.2
  37.7 0.0 copy-start
  37.7 1.0 %shard_map.102 = (f32[16,128,128]{2,1,0:T(8,128)S(1)}, bf16[16,128,128]{2,1,0:T(8,128)(2,1)S(1)}, bf16[512,128]{1,0:T(8,128)(2,1)S(1)}, f32[128,128]{1,0:T(8,128)S(1)}) custom-call(bf16[2,16,80,128]{3,2,1,0:T(8,128)(2,1)S(1)} %bitcast.18, bf16[4,144,128]{2,1,0:T(8,128)(2,1)S(1)} %bitcast.20, f32[32,128]{1,0:T(8,128)S(1)} %copy-done.1, ...), custom_call_target="tpu_custom_call" | custom-call | flops 1000000000 | bytes 4000000 | tf_op jit(solution)/shard_map/pallas_call | solution.py:269
  38.7 1.3 %all-to-all-done = bf16[16,8,128]{2,1,0:T(8,128)(2,1)S(1)} async-done(((bf16[16,8,128]{2,1,0:T(8,128)(2,1)}), bf16[16,8,128]{2,1,0:T(8,128)(2,1)S(1)}, u32[]{:S(2)}, u32[]{:S(2)}) %all-to-all-start) | async-done | bytes 32800 | tf_op jit(solution)/shard_map/all_to_all | solution.py:266
  40.0 0.0 copy-done
  40.0 1.2 %shard_map.103 = bf16[512,128]{1,0:T(8,128)(2,1)S(1)} custom-call(bf16[128,128]{1,0:T(8,128)(2,1)S(1)} %bitcast.23, f32[16,128,128]{2,1,0:T(8,128)S(1)} %get-tuple-element.17.s_in, bf16[16,128,128]{2,1,0:T(8,128)(2,1)S(1)} %get-tuple-element.18.v, bf16[512,128]{1,0:T(8,128)(2,1)S(1)} %get-tuple-element.19.gate, f32[128,128]{1,0:T(8,128)S(1)} %get-tuple-element.20.moved, ...), custom_call_target="tpu_custom_call" | custom-call | flops 100000000 | bytes 3000000 | tf_op jit(solution)/shard_map/pallas_call | solution.py:277
  41.2 19.6 %all_to_all.15 = bf16[32,16,128]{2,1,0:T(8,128)(2,1)S(1)} all-to-all(bf16[32,16,128]{2,1,0:T(8,128)(2,1)S(1)} %bitcast.22), channel_id=1, replica_groups={{32,34,36,38,40,42,44,46,48,50,52,54,56,58,60,62,0,2,4,6,8,10,12,14,16,..., dimensions={0} | all-to-all | bytes 262144 | tf_op jit(solution)/shard_map/all_to_all | solution.py:285
  60.8 0.8 %shard_map.104 = bf16[512,128]{1,0:T(8,128)(2,1)} custom-call(bf16[512,128]{1,0:T(8,128)(2,1)S(1)} %bitcast.21), custom_call_target="tpu_custom_call" | custom-call | bytes 300000 | tf_op jit(solution)/shard_map/pallas_call | solution.py:288
Async XLA Ops:
  2.7 7.6 %copy-start.3 = (bf16[144,128]{1,0:T(8,128)(2,1)S(1)}, bf16[144,128]{1,0:T(8,128)(2,1)}, u32[]{:S(2)}) copy-start(bf16[144,128]{1,0:T(8,128)(2,1)} %get-tuple-element.13) | copy-start | bytes 110596
  2.7 17.3 %all-to-all-start.1 = ((bf16[16,80,128]{2,1,0:T(8,128)(2,1)}), bf16[16,80,128]{2,1,0:T(8,128)(2,1)S(1)}, u32[]{:S(2)}, u32[]{:S(2)}) async-start(bf16[16,80,128]{2,1,0:T(8,128)(2,1)} %bitcast.24), calls=%async_computation.1 | async-start | bytes 655360 | tf_op jit(solution)/shard_map/all_to_all | solution.py:260
  20.0 20.0 %all-to-all-start = ((bf16[16,8,128]{2,1,0:T(8,128)(2,1)}), bf16[16,8,128]{2,1,0:T(8,128)(2,1)S(1)}, u32[]{:S(2)}, u32[]{:S(2)}) async-start(bf16[16,8,128]{2,1,0:T(8,128)(2,1)} %bitcast.10), calls=%async_computation | async-start | bytes 65536 | tf_op jit(solution)/shard_map/all_to_all | solution.py:266
  34.9 2.8 %copy-start.1 = (f32[32,128]{1,0:T(8,128)S(1)}, f32[32,128]{1,0:T(8,128)}, u32[]{:S(2)}) copy-start(f32[32,128]{1,0:T(8,128)} %get-tuple-element.15.same) | copy-start | bytes 49156
  34.9 2.8 %copy-start.2 = (bf16[32,128]{1,0:T(8,128)(2,1)S(1)}, bf16[32,128]{1,0:T(8,128)(2,1)}, u32[]{:S(2)}) copy-start(bf16[32,128]{1,0:T(8,128)(2,1)} %get-tuple-element.16.sel) | copy-start | bytes 24580
  37.7 2.3 %copy-start = (bf16[128,128]{1,0:T(8,128)(2,1)S(1)}, bf16[128,128]{1,0:T(8,128)(2,1)}, u32[]{:S(2)}) copy-start(bf16[128,128]{1,0:T(8,128)(2,1)} %w_out.1) | copy-start | bytes 98308

commit v8 on v7

--- a/solution.py
+++ b/solution.py
@@ -172,7 +172,7 @@
         v_out[i] = kv[128:256]
         zq_scr[i * Q : (i + 1) * Q] = nt(selector, zt).astype(BF16)
     qg = nt(zq_scr[...], w_qg).astype(BF16)
-    gate_out[...] = qg[:, 128:256]
+    gate_out[...] = jax.nn.sigmoid(qg[:, 128:256].astype(F32))
     head_of_lane = iota((Q, 128), 1) // HD
     moved_out[...] = jnp.concatenate(
         [same[...] * (small[4 + k : 5 + k] + small[8 + k : 9 + k] + small[12 + k : 13 + k]) for k in range(HEADS)], axis=0
@@ -199,7 +199,7 @@
         o = every[0:Q]
         for k in range(1, HEADS):
             o = jnp.where(head_of_lane == k, every[k * Q : (k + 1) * Q], o)
-        acc[pl.ds((i // 2 ^ away) * 2 + i % 2, Q, stride=I), :] = jax.nn.sigmoid(gate[i * Q : (i + 1) * Q, :].astype(F32)) * o
+        acc[pl.ds((i // 2 ^ away) * 2 + i % 2, Q, stride=I), :] = gate[i * Q : (i + 1) * Q, :] * o
     out[...] = nn(acc[...].astype(BF16), w_out[...]).astype(BF16)
 
 
@@ -269,7 +269,7 @@
     scores, v, gate, moved = call(
         score_kernel,
         [VMEM] * 4,
-        [shape((I, 128, 128), F32), shape((I, 128, 128), BF16), shape((I * Q, 128), BF16), shape((128, 128), F32)],
+        [shape((I, 128, 128), F32), shape((I, 128, 128), BF16), shape((I * Q, 128), F32), shape((128, 128), F32)],
         [pltpu.VMEM((I * Q, 128), BF16), pltpu.VMEM((I, 128, 128), BF16)],
         flops=1000000000,
         nbytes=4000000,

time: 62 us -> 62 us (level)
  no operation moved by 1% of the time
where the time goes in v8:
time: 62 us; the launch traced here: 61.6 us
  blocking collectives  31.3 us (50%)
  starting transfers between devices  22.5 us (36%)
  Pallas kernels  5.75 us (9%)
  waiting for transfers between devices  1.29 us (2%)
  between operations  0.71 us (1%)
    all_to_all x1, blocking collectives, local(): lax.all_to_all(mixed.reshape(32, I, 128), ('row', 'head'), 0, 0, tiled=Tr...  19.6 us
    all_to_all x1, starting transfers between devices, local(): lax.all_to_all(mine.reshape(16, 8, 128), ('row', 'head'), 0, 0, tiled=Tru...  14.9 us
    all_gather x1, blocking collectives, local(): near = lax.all_gather(near, 'head', axis=0)  8.96 us
    all_to_all x1, starting transfers between devices, local(): lax.all_to_all(packed.reshape(16, MSG, 128), ('row', 'head'), 0, 0, tiled...  7.6 us
    all_gather x1, blocking collectives, local(): g = lax.all_gather(got, 'head', axis=0, axis_index_groups=OVER_CORE)  2.76 us
    pallas_call x1, Pallas kernels, local(): pl.pallas_call(pack_kernel, in_specs=[HBM] * 9, out_specs=[HBM] * 4, out_...  1.99 us
    all_to_all x1, waiting for transfers between devices, local(): lax.all_to_all(mine.reshape(16, 8, 128), ('row', 'head'), 0, 0, tiled=Tru...  1.29 us
  transfers between devices with their start and end apart: 2, of which 1 were waited for; matrix products, arithmetic and copies ran while one was open for 0% of the time, Pallas kernels for 3%

profile of v8, /device:TPU:1, one launch (start us, length us, event | category | flops | bytes accessed | tf_op | source)
XLA Modules:
  0.0 61.6 jit_solution(18152275687078916463)
XLA Ops:
  0.7 2.0 %shard_map.100 = (bf16[1280,128]{1,0:T(8,128)(2,1)}, bf16[144,128]{1,0:T(8,128)(2,1)}, f32[32,128]{1,0:T(8,128)}, bf16[32,128]{1,0:T(8,128)(2,1)}) custom-call(bf16[4,32,512]{2,1,0:T(8,128)(2,1)} %bitcast.25, bf16[32,128]{1,0:T(8,128)(2,1)} %bitcast.26, bf16[32,128]{1,0:T(8,128)(2,1)} %bitcast.27, bf16[32,128]{1,0:T(8,128)(2,1)} %bitcast.28, ...), custom_call_target="tpu_custom_call" | custom-call | bytes 1000000 | tf_op jit(solution)/shard_map/pallas_call | solution.py:236
  2.7 0.0 copy-start.3
  2.7 7.6 %all-to-all-start.1 = ((bf16[16,80,128]{2,1,0:T(8,128)(2,1)}), bf16[16,80,128]{2,1,0:T(8,128)(2,1)S(1)}, u32[]{:S(2)}, u32[]{:S(2)}) async-start(bf16[16,80,128]{2,1,0:T(8,128)(2,1)} %bitcast.24), calls=%async_computation.1 | async-start | bytes 655360 | tf_op jit(solution)/shard_map/all_to_all | solution.py:260
  10.3 0.0 copy-done.3
  10.3 9.0 %all-gather = bf16[576,128]{1,0:T(8,128)(2,1)S(1)} all-gather(bf16[144,128]{1,0:T(8,128)(2,1)S(1)} %copy-done.3), channel_id=2, replica_groups=mesh['row'=128,'head'=4] {'head'}, dimensions={0}, use_global_device_ids=true | all-gather | bytes 184320 | tf_op jit(solution)/shard_map/all_gather | solution.py:264
  19.2 0.8 %shard_map.101 = bf16[128,128]{1,0:T(8,128)(2,1)} custom-call(bf16[4,144,128]{2,1,0:T(8,128)(2,1)S(1)} %bitcast.19), custom_call_target="tpu_custom_call" | custom-call | bytes 400000 | tf_op jit(solution)/shard_map/pallas_call | solution.py:265
  20.0 0.0 all-to-all-done.1
  20.0 14.9 %all-to-all-start = ((bf16[16,8,128]{2,1,0:T(8,128)(2,1)}), bf16[16,8,128]{2,1,0:T(8,128)(2,1)S(1)}, u32[]{:S(2)}, u32[]{:S(2)}) async-start(bf16[16,8,128]{2,1,0:T(8,128)(2,1)} %bitcast.10), calls=%async_computation | async-start | bytes 65536 | tf_op jit(solution)/shard_map/all_to_all | solution.py:266
  34.9 0.0 copy-start.1
  34.9 0.0 copy-start.2
  34.9 2.8 %all-gather.1 = bf16[32,80,128]{2,1,0:T(8,128)(2,1)S(1)} all-gather(bf16[16,80,128]{2,1,0:T(8,128)(2,1)S(1)} %all-to-all-done.1), channel_id=3, replica_groups={{0,1},{2,3},{4,5},{6,7},{8,9},{10,11},{12,13},{14,15},{16,17},{18,19},{..., dimensions={0}, use_global_device_ids=true | all-gather | bytes 983040 | tf_op jit(solution)/shard_map/all_gather | solution.py:263
  37.7 0.0 copy-done.1
  37.7 0.0 copy-done.2
  37.7 0.0 copy-start
  37.7 1.0 %shard_map.102 = (f32[16,128,128]{2,1,0:T(8,128)S(1)}, bf16[16,128,128]{2,1,0:T(8,128)(2,1)S(1)}, f32[512,128]{1,0:T(8,128)S(1)}, f32[128,128]{1,0:T(8,128)S(1)}) custom-call(bf16[2,16,80,128]{3,2,1,0:T(8,128)(2,1)S(1)} %bitcast.18, bf16[4,144,128]{2,1,0:T(8,128)(2,1)S(1)} %bitcast.20, f32[32,128]{1,0:T(8,128)S(1)} %copy-done.1, bf16[32,128]{1,0:T(8,128)(2,1)S(1)} %copy-done.2), custom_call_target="tpu_custom_call" | custom-call | flops 1000000000 | bytes 4000000 | tf_op jit(solution)/shard_map/pallas_call | solution.py:269
  38.7 1.3 %all-to-all-done = bf16[16,8,128]{2,1,0:T(8,128)(2,1)S(1)} async-done(((bf16[16,8,128]{2,1,0:T(8,128)(2,1)}), bf16[16,8,128]{2,1,0:T(8,128)(2,1)S(1)}, u32[]{:S(2)}, u32[]{:S(2)}) %all-to-all-start) | async-done | bytes 32800 | tf_op jit(solution)/shard_map/all_to_all | solution.py:266
  40.0 0.0 copy-done
  40.0 1.2 %shard_map.103 = bf16[512,128]{1,0:T(8,128)(2,1)S(1)} custom-call(bf16[128,128]{1,0:T(8,128)(2,1)S(1)} %bitcast.23, f32[16,128,128]{2,1,0:T(8,128)S(1)} %get-tuple-element.17.s_in, bf16[16,128,128]{2,1,0:T(8,128)(2,1)S(1)} %get-tuple-element.18.v, f32[512,128]{1,0:T(8,128)S(1)} %get-tuple-element.19.gate, f32[128,128]{1,0:T(8,128)S(1)} %get-tuple-element.20.moved, ...), custom_call_target="tpu_custom_call" | custom-call | flops 100000000 | bytes 3000000 | tf_op jit(solution)/shard_map/pallas_call | solution.py:277
  41.2 19.6 %all_to_all.15 = bf16[32,16,128]{2,1,0:T(8,128)(2,1)S(1)} all-to-all(bf16[32,16,128]{2,1,0:T(8,128)(2,1)S(1)} %bitcast.21), channel_id=1, replica_groups={{32,34,36,38,40,42,44,46,48,50,52,54,56,58,60,62,0,2,4,6,8,10,12,14,16,..., dimensions={0} | all-to-all | bytes 262144 | tf_op jit(solution)/shard_map/all_to_all | solution.py:285
  60.8 0.8 %shard_map.104 = bf16[512,128]{1,0:T(8,128)(2,1)} custom-call(bf16[512,128]{1,0:T(8,128)(2,1)S(1)} %bitcast.22), custom_call_target="tpu_custom_call" | custom-call | bytes 300000 | tf_op jit(solution)/shard_map/pallas_call | solution.py:288
Async XLA Ops:
  2.7 7.6 %copy-start.3 = (bf16[144,128]{1,0:T(8,128)(2,1)S(1)}, bf16[144,128]{1,0:T(8,128)(2,1)}, u32[]{:S(2)}) copy-start(bf16[144,128]{1,0:T(8,128)(2,1)} %get-tuple-element.13) | copy-start | bytes 110596
  2.7 17.3 %all-to-all-start.1 = ((bf16[16,80,128]{2,1,0:T(8,128)(2,1)}), bf16[16,80,128]{2,1,0:T(8,128)(2,1)S(1)}, u32[]{:S(2)}, u32[]{:S(2)}) async-start(bf16[16,80,128]{2,1,0:T(8,128)(2,1)} %bitcast.24), calls=%async_computation.1 | async-start | bytes 655360 | tf_op jit(solution)/shard_map/all_to_all | solution.py:260
  20.0 20.0 %all-to-all-start = ((bf16[16,8,128]{2,1,0:T(8,128)(2,1)}), bf16[16,8,128]{2,1,0:T(8,128)(2,1)S(1)}, u32[]{:S(2)}, u32[]{:S(2)}) async-start(bf16[16,8,128]{2,1,0:T(8,128)(2,1)} %bitcast.10), calls=%async_computation | async-start | bytes 65536 | tf_op jit(solution)/shard_map/all_to_all | solution.py:266
  34.9 2.8 %copy-start.1 = (f32[32,128]{1,0:T(8,128)S(1)}, f32[32,128]{1,0:T(8,128)}, u32[]{:S(2)}) copy-start(f32[32,128]{1,0:T(8,128)} %get-tuple-element.15.same) | copy-start | bytes 49156
  34.9 2.8 %copy-start.2 = (bf16[32,128]{1,0:T(8,128)(2,1)S(1)}, bf16[32,128]{1,0:T(8,128)(2,1)}, u32[]{:S(2)}) copy-start(bf16[32,128]{1,0:T(8,128)(2,1)} %get-tuple-element.16.sel) | copy-start | bytes 24580
  37.7 2.3 %copy-start = (bf16[128,128]{1,0:T(8,128)(2,1)S(1)}, bf16[128,128]{1,0:T(8,128)(2,1)}, u32[]{:S(2)}) copy-start(bf16[128,128]{1,0:T(8,128)(2,1)} %w_out.1) | copy-start | bytes 98308

commit v9 on v6

--- a/solution.py
+++ b/solution.py
@@ -144,11 +144,12 @@
 def bias_kernel(near, out):
     core = place()[2]
     small = heads_small(near).astype(BF16)
-    found = []
-    for y in range(2):
-        rows = pl.ds(pl.multiple_of((2 * y + core) * 32, 32), 32)
-        found.append(nn(small, jnp.concatenate([near[k, rows, :] for k in range(HEADS)], axis=0))[0:4])
-    tile = jnp.concatenate(found * 2, axis=0).astype(BF16)
+    z = [
+        jnp.concatenate([near[k, pl.ds(pl.multiple_of((2 * y + core) * 32, 32), 32), :] for k in range(HEADS)], axis=0)
+        for y in range(2)
+    ]
+    both = nn(small, jnp.concatenate(z, axis=1))[0:4]
+    tile = jnp.concatenate([both[:, 0:128], both[:, 128:256]] * 2, axis=0).astype(BF16)
     for r in range(8):
         out[r * 16 : (r + 1) * 16, :] = tile
 
@@ -172,7 +173,7 @@
         v_out[i] = kv[128:256]
         zq_scr[i * Q : (i + 1) * Q] = nt(selector, zt).astype(BF16)
     qg = nt(zq_scr[...], w_qg).astype(BF16)
-    gate_out[...] = qg[:, 128:256]
+    gate_out[...] = jax.nn.sigmoid(qg[:, 128:256].astype(F32))
     head_of_lane = iota((Q, 128), 1) // HD
     moved = jnp.concatenate(
         [same[...] * (small[4 + k : 5 + k] + small[8 + k : 9 + k] + small[12 + k : 13 + k]) for k in range(HEADS)], axis=0
@@ -199,7 +200,7 @@
         o = every[0:Q]
         for k in range(1, HEADS):
             o = jnp.where(head_of_lane == k, every[k * Q : (k + 1) * Q], o)
-        acc[pl.ds((i // 2 ^ away) * 2 + i % 2, Q, stride=I), :] = jax.nn.sigmoid(gate[i * Q : (i + 1) * Q, :].astype(F32)) * o
+        acc[pl.ds((i // 2 ^ away) * 2 + i % 2, Q, stride=I), :] = gate[i * Q : (i + 1) * Q, :] * o
     out[...] = nn(acc[...].astype(BF16), w_out[...]).astype(BF16)
 
 
@@ -269,7 +270,7 @@
     scores, v, gate = call(
         score_kernel,
         [VMEM] * 4,
-        [shape((I, 128, 128), F32), shape((I, 128, 128), BF16), shape((I * Q, 128), BF16)],
+        [shape((I, 128, 128), F32), shape((I, 128, 128), BF16), shape((I * Q, 128), F32)],
         [pltpu.VMEM((I * Q, 128), BF16), pltpu.VMEM((I, 128, 128), BF16)],
         flops=1000000000,
         nbytes=4000000,

time: 62 us -> 62 us (level)
  no operation moved by 1% of the time
where the time goes in v9:
time: 62 us; the launch traced here: 61.6 us
  blocking collectives  31.3 us (50%)
  starting transfers between devices  22.5 us (36%)
  Pallas kernels  5.75 us (9%)
  waiting for transfers between devices  1.29 us (2%)
  between operations  0.72 us (1%)
    all_to_all x1, blocking collectives, local(): lax.all_to_all(mixed.reshape(32, I, 128), ('row', 'head'), 0, 0, tiled=Tr...  19.6 us
    all_to_all x1, starting transfers between devices, local(): lax.all_to_all(mine.reshape(16, 8, 128), ('row', 'head'), 0, 0, tiled=Tru...  14.9 us
    all_gather x1, blocking collectives, local(): near = lax.all_gather(near, 'head', axis=0)  8.96 us
    all_to_all x1, starting transfers between devices, local(): lax.all_to_all(packed.reshape(16, MSG, 128), ('row', 'head'), 0, 0, tiled...  7.6 us
    all_gather x1, blocking collectives, local(): g = lax.all_gather(got, 'head', axis=0, axis_index_groups=OVER_CORE)  2.76 us
    pallas_call x1, Pallas kernels, local(): pl.pallas_call(pack_kernel, in_specs=[HBM] * 9, out_specs=[HBM] * 4, out_...  1.99 us
    all_to_all x1, waiting for transfers between devices, local(): lax.all_to_all(mine.reshape(16, 8, 128), ('row', 'head'), 0, 0, tiled=Tru...  1.29 us
  transfers between devices with their start and end apart: 2, of which 1 were waited for; matrix products, arithmetic and copies ran while one was open for 0% of the time, Pallas kernels for 3%

profile of v9, /device:TPU:1, one launch (start us, length us, event | category | flops | bytes accessed | tf_op | source)
XLA Modules:
  0.0 61.6 jit_solution(13976816686386118449)
XLA Ops:
  0.7 2.0 %shard_map.100 = (bf16[1280,128]{1,0:T(8,128)(2,1)}, bf16[144,128]{1,0:T(8,128)(2,1)}, f32[32,128]{1,0:T(8,128)}, bf16[32,128]{1,0:T(8,128)(2,1)}) custom-call(bf16[4,32,512]{2,1,0:T(8,128)(2,1)} %bitcast.25, bf16[32,128]{1,0:T(8,128)(2,1)} %bitcast.26, bf16[32,128]{1,0:T(8,128)(2,1)} %bitcast.27, bf16[32,128]{1,0:T(8,128)(2,1)} %bitcast.28, ...), custom_call_target="tpu_custom_call" | custom-call | bytes 1000000 | tf_op jit(solution)/shard_map/pallas_call | solution.py:237
  2.7 0.0 copy-start.3
  2.7 7.6 %all-to-all-start.1 = ((bf16[16,80,128]{2,1,0:T(8,128)(2,1)}), bf16[16,80,128]{2,1,0:T(8,128)(2,1)S(1)}, u32[]{:S(2)}, u32[]{:S(2)}) async-start(bf16[16,80,128]{2,1,0:T(8,128)(2,1)} %bitcast.24), calls=%async_computation.1 | async-start | bytes 655360 | tf_op jit(solution)/shard_map/all_to_all | solution.py:261
  10.3 0.0 copy-done.3
  10.3 9.0 %all-gather = bf16[576,128]{1,0:T(8,128)(2,1)S(1)} all-gather(bf16[144,128]{1,0:T(8,128)(2,1)S(1)} %copy-done.3), channel_id=2, replica_groups=mesh['row'=128,'head'=4] {'head'}, dimensions={0}, use_global_device_ids=true | all-gather | bytes 184320 | tf_op jit(solution)/shard_map/all_gather | solution.py:265
  19.2 0.8 %shard_map.101 = bf16[128,128]{1,0:T(8,128)(2,1)} custom-call(bf16[4,144,128]{2,1,0:T(8,128)(2,1)S(1)} %bitcast.19), custom_call_target="tpu_custom_call" | custom-call | bytes 400000 | tf_op jit(solution)/shard_map/pallas_call | solution.py:266
  20.0 0.0 all-to-all-done.1
  20.0 14.9 %all-to-all-start = ((bf16[16,8,128]{2,1,0:T(8,128)(2,1)}), bf16[16,8,128]{2,1,0:T(8,128)(2,1)S(1)}, u32[]{:S(2)}, u32[]{:S(2)}) async-start(bf16[16,8,128]{2,1,0:T(8,128)(2,1)} %bitcast.10), calls=%async_computation | async-start | bytes 65536 | tf_op jit(solution)/shard_map/all_to_all | solution.py:267
  34.9 0.0 copy-start.1
  34.9 0.0 copy-start.2
  34.9 2.8 %all-gather.1 = bf16[32,80,128]{2,1,0:T(8,128)(2,1)S(1)} all-gather(bf16[16,80,128]{2,1,0:T(8,128)(2,1)S(1)} %all-to-all-done.1), channel_id=3, replica_groups={{0,1},{2,3},{4,5},{6,7},{8,9},{10,11},{12,13},{14,15},{16,17},{18,19},{..., dimensions={0}, use_global_device_ids=true | all-gather | bytes 983040 | tf_op jit(solution)/shard_map/all_gather | solution.py:264
  37.7 0.0 copy-done.1
  37.7 0.0 copy-done.2
  37.7 0.0 copy-start
  37.7 1.0 %shard_map.102 = (f32[16,128,128]{2,1,0:T(8,128)S(1)}, bf16[16,128,128]{2,1,0:T(8,128)(2,1)S(1)}, f32[512,128]{1,0:T(8,128)S(1)}) custom-call(bf16[2,16,80,128]{3,2,1,0:T(8,128)(2,1)S(1)} %bitcast.18, bf16[4,144,128]{2,1,0:T(8,128)(2,1)S(1)} %bitcast.20, f32[32,128]{1,0:T(8,128)S(1)} %copy-done.1, bf16[32,128]{1,0:T(8,128)(2,1)S(1)} %copy-done.2), custom_call_target="tpu_custom_call" | custom-call | flops 1000000000 | bytes 4000000 | tf_op jit(solution)/shard_map/pallas_call | solution.py:270
  38.7 1.3 %all-to-all-done = bf16[16,8,128]{2,1,0:T(8,128)(2,1)S(1)} async-done(((bf16[16,8,128]{2,1,0:T(8,128)(2,1)}), bf16[16,8,128]{2,1,0:T(8,128)(2,1)S(1)}, u32[]{:S(2)}, u32[]{:S(2)}) %all-to-all-start) | async-done | bytes 32800 | tf_op jit(solution)/shard_map/all_to_all | solution.py:267
  40.0 0.0 copy-done
  40.0 1.2 %shard_map.103 = bf16[512,128]{1,0:T(8,128)(2,1)S(1)} custom-call(bf16[128,128]{1,0:T(8,128)(2,1)S(1)} %bitcast.23, f32[16,128,128]{2,1,0:T(8,128)S(1)} %get-tuple-element.16.s_in, bf16[16,128,128]{2,1,0:T(8,128)(2,1)S(1)} %get-tuple-element.17.v, f32[512,128]{1,0:T(8,128)S(1)} %get-tuple-element.18.gate, bf16[128,128]{1,0:T(8,128)(2,1)S(1)} %copy-done), custom_call_target="tpu_custom_call" | custom-call | flops 100000000 | bytes 3000000 | tf_op jit(solution)/shard_map/pallas_call | solution.py:278
  41.2 19.6 %all_to_all.15 = bf16[32,16,128]{2,1,0:T(8,128)(2,1)S(1)} all-to-all(bf16[32,16,128]{2,1,0:T(8,128)(2,1)S(1)} %bitcast.21), channel_id=1, replica_groups={{32,34,36,38,40,42,44,46,48,50,52,54,56,58,60,62,0,2,4,6,8,10,12,14,16,..., dimensions={0} | all-to-all | bytes 262144 | tf_op jit(solution)/shard_map/all_to_all | solution.py:286
  60.8 0.8 %shard_map.104 = bf16[512,128]{1,0:T(8,128)(2,1)} custom-call(bf16[512,128]{1,0:T(8,128)(2,1)S(1)} %bitcast.22), custom_call_target="tpu_custom_call" | custom-call | bytes 300000 | tf_op jit(solution)/shard_map/pallas_call | solution.py:289
Async XLA Ops:
  2.7 7.6 %copy-start.3 = (bf16[144,128]{1,0:T(8,128)(2,1)S(1)}, bf16[144,128]{1,0:T(8,128)(2,1)}, u32[]{:S(2)}) copy-start(bf16[144,128]{1,0:T(8,128)(2,1)} %get-tuple-element.12) | copy-start | bytes 110596
  2.7 17.3 %all-to-all-start.1 = ((bf16[16,80,128]{2,1,0:T(8,128)(2,1)}), bf16[16,80,128]{2,1,0:T(8,128)(2,1)S(1)}, u32[]{:S(2)}, u32[]{:S(2)}) async-start(bf16[16,80,128]{2,1,0:T(8,128)(2,1)} %bitcast.24), calls=%async_computation.1 | async-start | bytes 655360 | tf_op jit(solution)/shard_map/all_to_all | solution.py:261
  20.0 20.0 %all-to-all-start = ((bf16[16,8,128]{2,1,0:T(8,128)(2,1)}), bf16[16,8,128]{2,1,0:T(8,128)(2,1)S(1)}, u32[]{:S(2)}, u32[]{:S(2)}) async-start(bf16[16,8,128]{2,1,0:T(8,128)(2,1)} %bitcast.10), calls=%async_computation | async-start | bytes 65536 | tf_op jit(solution)/shard_map/all_to_all | solution.py:267
  34.9 2.8 %copy-start.1 = (f32[32,128]{1,0:T(8,128)S(1)}, f32[32,128]{1,0:T(8,128)}, u32[]{:S(2)}) copy-start(f32[32,128]{1,0:T(8,128)} %get-tuple-element.14.same) | copy-start | bytes 49156
  34.9 2.8 %copy-start.2 = (bf16[32,128]{1,0:T(8,128)(2,1)S(1)}, bf16[32,128]{1,0:T(8,128)(2,1)}, u32[]{:S(2)}) copy-start(bf16[32,128]{1,0:T(8,128)(2,1)} %get-tuple-element.15.sel) | copy-start | bytes 24580
  37.7 2.3 %copy-start = (bf16[128,128]{1,0:T(8,128)(2,1)S(1)}, bf16[128,128]{1,0:T(8,128)(2,1)}, u32[]{:S(2)}) copy-start(bf16[128,128]{1,0:T(8,128)(2,1)} %w_out.1) | copy-start | bytes 98308
